TPU v7x, 128 devices: a whole 4x4x4 slice. The times are simulated.
128 devices in a mesh: row: 8 (over z, x_hi), col: 16 (over y, x_lo, core).
Axes of the slice: x: 4 (x_hi: 2, x_lo: 2; x = x_hi * 2 + x_lo), y: 4, z: 4, core: 2. Of those that a mesh axis runs over, the one named last changes fastest.
Arguments:
- inputs: bfloat16 [1024, 12288], P(('row', 'col')), may hold values from -24 to 24
- cotangent: bfloat16 [1024, 12288], P('row', 'col'), may hold values from -6 to 6
- w_in: bfloat16 [12288, 24576], P('col', 'row'), may hold values from -0.109375 to 0.109375
- w_out: bfloat16 [24576, 12288], P('row', 'col'), may hold values from -0.078125 to 0.078125
- mask_in: int32 [192, 384], P('col', 'row'), may hold values 0 or 1
- mask_out: int32 [384, 192], P('row', 'col'), may hold values 0 or 1
Outputs:
- output: bfloat16 [1024, 12288], P('row', 'col')
- input_grad: bfloat16 [1024, 12288], P('row', 'col')
- w_in_grad: bfloat16 [12288, 24576], P('col', 'row')
- w_out_grad: bfloat16 [24576, 12288], P('row', 'col')
All inputs are finite; a program needn't handle non-finite values. No bound on the sum of `mask_in` or of `mask_out` on one device may be relied on, other than what follows from the above.
Results may differ from a plain program's by a relative error of at most 0.0051.
Values may be sent and summed in bfloat16 or wider, within the bound.
A program may use at most 192 MiB of HBM per device.

v0:
```python
import jax
import jax.numpy as jnp
from jax import lax
from jax.sharding import PartitionSpec as P


def masked(weight, blocks):
    block_rows, block_cols = blocks.shape
    shaped = weight.reshape(
        block_rows, weight.shape[0] // block_rows, block_cols, weight.shape[1] // block_cols
    )
    return (shaped * blocks.astype(weight.dtype)[:, None, :, None]).reshape(weight.shape)


def gelu_tanh(values):
    return jax.nn.gelu(values, approximate=True)


def gelu_back(hidden, act_grad):
    unused, pullback = jax.vjp(gelu_tanh, hidden)
    return pullback(act_grad)[0]


def product(operand, weight, contract):
    return lax.dot_general(
        operand, weight, (((1,), (contract,)), ((), ())), preferred_element_type=jnp.float32
    )


def body(inputs, cotangent, w_in, w_out, mask_in, mask_out):
    first = masked(w_in, mask_in)
    second = masked(w_out, mask_out)
    feature = lax.all_to_all(inputs, "col", split_axis=1, concat_axis=0, tiled=True)
    tokens_all, grads_all = (
        lax.all_gather(feature, "row", axis=0, tiled=True),
        lax.all_gather(cotangent, "row", axis=0, tiled=True),
    )

    def col_sum(operand, weight, contract):
        return lax.psum_scatter(
            product(operand, weight, contract), "col", scatter_dimension=0, tiled=True
        )

    def col_gather(values):
        return lax.all_gather(values, "col", axis=0, tiled=True)

    def row_sum(operand, weight, contract):
        return lax.psum_scatter(
            product(operand, weight, contract), "row", scatter_dimension=0, tiled=True
        )

    hidden = col_sum(tokens_all, first, 0)
    activated_all = col_gather(gelu_tanh(hidden).astype(jnp.bfloat16))
    output = row_sum(activated_all, second, 0).astype(jnp.bfloat16)
    act_grad = col_sum(grads_all, second, 1)
    hidden_grad_all = col_gather(gelu_back(hidden, act_grad).astype(jnp.bfloat16))
    input_grad = row_sum(hidden_grad_all, first, 1).astype(jnp.bfloat16)
    in_product = lax.dot_general(
        tokens_all, hidden_grad_all, (((0,), (0,)), ((), ())), preferred_element_type=jnp.float32
    )
    w_in_grad = masked(in_product, mask_in).astype(jnp.bfloat16)
    out_product = lax.dot_general(
        activated_all, grads_all, (((0,), (0,)), ((), ())), preferred_element_type=jnp.float32
    )
    w_out_grad = masked(out_product, mask_out).astype(jnp.bfloat16)
    return (output, input_grad, w_in_grad, w_out_grad)


def solution(mesh):
    in_specs = (
        P(("row", "col"), None),
        P("row", "col"),
        P("col", "row"),
        P("row", "col"),
        P("col", "row"),
        P("row", "col"),
    )
    out_specs = (P("row", "col"), P("row", "col"), P("col", "row"), P("row", "col"))
    return jax.shard_map(body, mesh=mesh, in_specs=in_specs, out_specs=out_specs, check_vma=False)
```

profile of v0, /device:TPU:0, one launch (start us, length us, event | category | flops | bytes accessed | tf_op | source)
XLA Modules:
  0.0 659.3 jit_solution(18149769726580120072)
XLA Ops:
  7.9 13.1 %all_to_all.19 = bf16[8,16,768]{2,0,1:T(8,128)(2,1)} all-to-all(bf16[8,16,768]{2,0,1:T(8,128)(2,1)} %bitcast.37), channel_id=1, replica_groups=mesh['row'=8,'col'=16] {'col'}, dimensions={1} | all-to-all | bytes 393216 | tf_op jit(solution)/shard_map/all_to_all | solution.py:33
  21.1 6.6 %copy.29 = bf16[3072,768]{0,1:T(8,128)(2,1)} copy(bf16[3072,768]{1,0:T(8,128)(2,1)} %param.9) | data formatting | bytes 9437184 | tf_op args[3]
  27.8 4.9 mul.98
  32.7 12.5 %mul.99 = bf16[3072,768]{0,1:T(8,128)(2,1)} reshape(bf16[48,64,12,64]{1,0,3,2:T(8,128)(2,1)} %mul.98) | data formatting | bytes 9437184 | tf_op jit(solution)/shard_map/mul | solution.py:12
  45.2 17.2 %all-gather.9.cloned.1.call-done = bf16[1024,768]{1,0:T(8,128)(2,1)} async-done(((bf16[128,768]{1,0:T(8,128)(2,1)}), bf16[1024,768]{1,0:T(8,128)(2,1)}) %all-gather.9.cloned.1.call-update) | async-done | bytes 1572880 | tf_op jit(solution)/shard_map/all_gather | solution.py:36
  62.5 11.0 %convolution_bitcast_fusion = f32[1024,3072]{0,1:T(8,128)} fusion(bf16[1024,768]{1,0:T(8,128)(2,1)} %all-gather.9.cloned.1.call-done, bf16[3072,768]{0,1:T(8,128)(2,1)} %copy.29, bf16[3072,768]{0,1:T(8,128)(2,1)} %mul.99), kind=kOutput, calls=%fused_computation.3 | convolution fusion | flops 4834197504 | bytes 23592960 | tf_op jit(solution)/shard_map/dot_general | solution.py:25
  73.4 12.7 %copy.38 = f32[1024,3072]{1,0:T(8,128)} copy(f32[1024,3072]{0,1:T(8,128)} %convolution_bitcast_fusion) | data formatting | bytes 25165824
  86.8 4.8 mul.91
  91.6 12.6 %mul.92 = bf16[768,3072]{1,0:T(8,128)(2,1)} reshape(bf16[12,64,48,64]{3,2,1,0:T(8,128)(2,1)} %mul.91) | data formatting | bytes 9437184 | tf_op jit(solution)/shard_map/mul | solution.py:12
  104.3 7.9 %mul.93 = bf16[768,3072]{1,0:T(8,128)(2,1)} multiply(bf16[768,3072]{1,0:T(8,128)(2,1)} %param.8, bf16[768,3072]{1,0:T(8,128)(2,1)} %mul.92) | non-fusion elementwise | flops 2359296 | bytes 14155776 | tf_op jit(solution)/shard_map/mul | solution.py:12
  112.2 0.9 all-gather.5.cloned.1.call-done
  113.1 10.7 %convolution_bitcast_fusion.1 = f32[1024,3072]{0,1:T(8,128)} fusion(bf16[768,3072]{1,0:T(8,128)(2,1)} %mul.93, bf16[1024,768]{1,0:T(8,128)(2,1)} %all-gather.5.cloned.1.call-done), kind=kOutput, calls=%fused_computation.4 | convolution fusion | flops 4831838208 | bytes 18874368 | tf_op jit(solution)/shard_map/dot_general | solution.py:25
  123.9 12.7 %copy.36 = f32[1024,3072]{1,0:T(8,128)} copy(f32[1024,3072]{0,1:T(8,128)} %convolution_bitcast_fusion.1) | data formatting | bytes 25165824
  136.6 117.7 %reduce-scatter.15.cloned.1.call-done = f32[64,3072]{1,0:T(8,128)} async-done(((f32[1024,3072]{1,0:T(8,128)}), f32[64,3072]{1,0:T(8,128)}) %reduce-scatter.15.cloned.1.call-update) | async-done | bytes 786448 | tf_op jit(solution)/shard_map/reduce_scatter | solution.py:40
  254.4 141.2 %reduce-scatter.13.cloned.1.call-done = f32[64,3072]{1,0:T(8,128)} async-done(((f32[1024,3072]{1,0:T(8,128)}), f32[64,3072]{1,0:T(8,128)}) %reduce-scatter.13.cloned.1.call-update) | async-done | bytes 786448 | tf_op jit(solution)/shard_map/reduce_scatter | solution.py:40
  395.5 2.9 fusion.10
  399.0 40.6 %all-gather.11.cloned.1.call-done = bf16[1024,3072]{1,0:T(8,128)(2,1)} async-done(((bf16[64,3072]{1,0:T(8,128)(2,1)}), bf16[1024,3072]{1,0:T(8,128)(2,1)}) %all-gather.11.cloned.1.call-update) | async-done | bytes 6291472 | tf_op jit(solution)/shard_map/all_gather | solution.py:45
  439.6 9.7 %fusion.13 = f32[1024,768]{1,0:T(8,128)} fusion(bf16[1024,3072]{1,0:T(8,128)(2,1)} %all-gather.11.cloned.1.call-done, bf16[768,3072]{1,0:T(8,128)(2,1)} %mul.93), kind=kOutput, calls=%fused_computation.20 | convolution fusion | flops 4831838208 | bytes 14155776 | tf_op jit(solution)/shard_map/dot_general | solution.py:25
  449.6 34.8 %all-gather.7.cloned.1.call-done = bf16[1024,3072]{1,0:T(8,128)(2,1)} async-done(((bf16[64,3072]{1,0:T(8,128)(2,1)}), bf16[1024,3072]{1,0:T(8,128)(2,1)}) %all-gather.7.cloned.1.call-update) | async-done | bytes 6291472 | tf_op jit(solution)/shard_map/all_gather | solution.py:45
  484.4 11.1 %fusion.2 = f32[1024,768]{1,0:T(8,128)} fusion(bf16[1024,3072]{1,0:T(8,128)(2,1)} %all-gather.7.cloned.1.call-done, bf16[3072,768]{0,1:T(8,128)(2,1)} %copy.29, bf16[3072,768]{0,1:T(8,128)(2,1)} %mul.99), kind=kOutput, calls=%fused_computation.6 | convolution fusion | flops 4834197504 | bytes 18874368 | tf_op jit(solution)/shard_map/dot_general | solution.py:25
  495.5 7.8 %mul.115 = f32[48,64,12,64]{1,0,3,2:T(8,128)} broadcast(f32[48,12]{0,1:T(8,128)S(1)} %get-tuple-element.22), dimensions={0,2} | broadcast | bytes 9439488 | tf_op jit(solution)/shard_map/mul | solution.py:12
  503.3 15.6 %mul.116 = f32[3072,768]{0,1:T(8,128)} reshape(f32[48,64,12,64]{1,0,3,2:T(8,128)} %mul.115) | data formatting | bytes 18874368 | tf_op jit(solution)/shard_map/mul | solution.py:12
  518.9 9.7 %copy.34 = f32[3072,768]{1,0:T(8,128)} copy(f32[3072,768]{0,1:T(8,128)} %mul.116) | data formatting | bytes 18874368 | tf_op jit(solution)/shard_map/mul | solution.py:12
  528.6 7.8 %mul.112 = f32[12,64,48,64]{3,2,1,0:T(8,128)} broadcast(f32[12,48]{1,0:T(8,128)S(1)} %get-tuple-element.24), dimensions={0,2} | broadcast | bytes 9439488 | tf_op jit(solution)/shard_map/mul | solution.py:12
  536.3 15.6 %mul.113 = f32[768,3072]{1,0:T(8,128)} reshape(f32[12,64,48,64]{3,2,1,0:T(8,128)} %mul.112) | data formatting | bytes 18874368 | tf_op jit(solution)/shard_map/mul | solution.py:12
  551.9 9.8 %copy.33 = f32[768,3072]{0,1:T(8,128)} copy(f32[768,3072]{1,0:T(8,128)} %mul.113) | data formatting | bytes 18874368 | tf_op jit(solution)/shard_map/mul | solution.py:12
  561.7 11.5 %fusion = bf16[768,3072]{0,1:T(8,128)(2,1)} fusion(f32[768,3072]{0,1:T(8,128)} %copy.33, bf16[1024,3072]{1,0:T(8,128)(2,1)} %all-gather.11.cloned.1.call-done, bf16[1024,768]{1,0:T(8,128)(2,1)S(1)} %copy-done.3), kind=kOutput, calls=%fused_computation.1 | convolution fusion | flops 4836556800 | bytes 22020096 | tf_op jit(solution)/shard_map/dot_general | solution.py:58
  573.2 6.7 %copy.35 = bf16[768,3072]{1,0:T(8,128)(2,1)} copy(bf16[768,3072]{0,1:T(8,128)(2,1)} %fusion) | data formatting | bytes 9437184
  579.9 11.6 %multiply_convert_fusion = bf16[3072,768]{1,0:T(8,128)(2,1)} fusion(f32[3072,768]{1,0:T(8,128)} %copy.34, bf16[1024,3072]{1,0:T(8,128)(2,1)} %all-gather.7.cloned.1.call-done, bf16[1024,768]{1,0:T(8,128)(2,1)S(1)} %copy-done.2), kind=kOutput, calls=%fused_computation.2 | convolution fusion | flops 4836556800 | bytes 22020096 | tf_op jit(solution)/shard_map/dot_general | solution.py:62
  591.5 1.7 convert_element_type.35
  593.2 57.5 %reduce-scatter.9.cloned.1.call-done = f32[128,768]{1,0:T(8,128)} async-done(((f32[1024,768]{1,0:T(8,128)}), f32[128,768]{1,0:T(8,128)}) %reduce-scatter.9.cloned.1.call-update) | async-done | bytes 393232 | tf_op jit(solution)/shard_map/reduce_scatter | solution.py:48
  650.7 1.7 convert_element_type.33
  (27 shorter events, 2.5 us)
Async XLA Ops:
  7.2 55.3 %all-gather.9.cloned.1.call-start = ((), (), s32[]{:S(2)}) async-start(), calls=%async_computation.8 | async-start | bytes 1769472 | tf_op jit(solution)/shard_map/all_gather | solution.py:36
  7.9 105.2 %all-gather.5.cloned.1.call-start = ((), (), s32[]{:S(2)}) async-start(), calls=%async_computation.5 | async-start | bytes 1769472 | tf_op jit(solution)/shard_map/all_gather | solution.py:35
  21.0 6.7 %copy-start = (s32[48,12]{0,1:T(8,128)S(1)}, s32[48,12]{0,1:T(8,128)}, u32[]{:S(2)}) copy-start(s32[48,12]{0,1:T(8,128)} %param.11) | copy-start | bytes 6916
  21.1 233.3 %reduce-scatter.15.cloned.1.call-start = ((), (), s32[]{:S(2)}) async-start(), calls=%async_computation.12 | async-start | bytes 13369344 | tf_op jit(solution)/shard_map/reduce_scatter | solution.py:40
  86.1 0.7 copy-start.1
  86.1 309.4 %reduce-scatter.13.cloned.1.call-start = ((), (), s32[]{:S(2)}) async-start(), calls=%async_computation.11 | async-start | bytes 13369344 | tf_op jit(solution)/shard_map/reduce_scatter | solution.py:40
  136.6 303.0 %all-gather.11.cloned.1.call-start = ((), (), s32[]{:S(2)}) async-start(), calls=%async_computation.9 | async-start | bytes 6684672 | tf_op jit(solution)/shard_map/all_gather | solution.py:45
  398.4 86.0 %all-gather.7.cloned.1.call-start = ((), (), s32[]{:S(2)}) async-start(), calls=%async_computation.6 | async-start | bytes 6684672 | tf_op jit(solution)/shard_map/all_gather | solution.py:45
  399.0 192.5 %reduce-scatter.11.cloned.1.call-start = ((), (), s32[]{:S(2)}) async-start(), calls=%async_computation.10 | async-start | bytes 3538944 | tf_op jit(solution)/shard_map/reduce_scatter | solution.py:48
  449.3 201.4 %reduce-scatter.9.cloned.1.call-start = ((), (), s32[]{:S(2)}) async-start(), calls=%async_computation.7 | async-start | bytes 3538944 | tf_op jit(solution)/shard_map/reduce_scatter | solution.py:48
  551.9 9.8 %copy-start.3 = (bf16[1024,768]{1,0:T(8,128)(2,1)S(1)}, bf16[1024,768]{1,0:T(8,128)(2,1)}, u32[]{:S(2)}) copy-start(bf16[1024,768]{1,0:T(8,128)(2,1)} %all-gather.5.cloned.1.call-done) | copy-start | bytes 4718596
  573.2 6.7 %copy-start.2 = (bf16[1024,768]{1,0:T(8,128)(2,1)S(1)}, bf16[1024,768]{1,0:T(8,128)(2,1)}, u32[]{:S(2)}) copy-start(bf16[1024,768]{1,0:T(8,128)(2,1)} %all-gather.9.cloned.1.call-done) | copy-start | bytes 4718596
Sparse Core Ops, SparseCore 0:
  10.3 52.1 all-gather.8
  64.8 48.3 all-gather.4
  115.6 138.7 reduce-scatter.14
  256.6 138.8 reduce-scatter.12
  398.5 41.0 all-gather.10
  441.2 43.1 all-gather.6
  488.2 80.3 reduce-scatter.10
  572.5 78.2 reduce-scatter.8
where the time goes:
time: 661 us; the launch traced here: 659 us
  waiting for transfers between devices  411 us (62%)
  local copies, waits for them, and re-layouts  140 us (21%)
  matrix products  65.5 us (10%)
  other arithmetic  14.2 us (2%)
  between operations  14.2 us (2%)
  blocking collectives  13.1 us (2%)
    reduce_scatter x2, waiting for transfers between devices, col_sum(): lax.psum_scatter(product(operand, weight, contract), 'col', scatter_dimen...  259 us
    mul x10, local copies, waits for them, and re-layouts, masked(): shaped * blocks.astype(weight.dtype)[:, None, :, None]  101 us
    all_gather x2, waiting for transfers between devices, col_gather(): return lax.all_gather(values, 'col', axis=0, tiled=True)  75.4 us
    reduce_scatter x2, waiting for transfers between devices, row_sum(): lax.psum_scatter(product(operand, weight, contract), 'row', scatter_dimen...  57.5 us
    dot_general x4, matrix products, product(): lax.dot_general(operand, weight, (((1,), (contract,)), ((), ())), preferr...  42.5 us
    unnamed x12, local copies, waits for them, and re-layouts  39.2 us
    all_gather x1, waiting for transfers between devices, body(): lax.all_gather(cotangent, 'row', axis=0, tiled=True)  17.2 us
  transfers between devices with their start and end apart: 8, of which 7 were waited for; matrix products, arithmetic and copies ran while one was open for 33% of the time, Pallas kernels for 0%

commit v1 on v0

v1 whole, which is shorter than its diff:
```python
import functools

import jax
import jax.numpy as jnp
from jax import lax
from jax.experimental import pallas as pl
from jax.experimental.pallas import tpu as pltpu
from jax.sharding import PartitionSpec as P

MESH = pl.DeviceIdType.MESH
F32 = jnp.float32
BF16 = jnp.bfloat16

GROUP = 128
GROUPS = 8
FEAT = 768
HALF = 1536
XW = 896
YW = HALF - XW
TILE = 256


def flip(position, by):
    return (position % 2 + by % 2) % 2 + 2 * ((position // 2 + by // 2) % 2)


def one_hot(shape, along, shift, offset):
    wide = lax.broadcasted_iota(jnp.int32, shape, along)
    other = lax.broadcasted_iota(jnp.int32, shape, 1 - along)
    return (lax.shift_right_logical(wide, shift) + offset == other).astype(F32).astype(BF16)


def gelu_parts(hidden, act_grad):
    c = 0.7978845608028654
    square = hidden * hidden
    inner = jnp.tanh(c * hidden * (1.0 + 0.044715 * square))
    cdf = 0.5 * (1.0 + inner)
    slope = cdf + 0.5 * hidden * (1.0 - inner * inner) * (c * (1.0 + 0.134145 * square))
    return hidden * cdf, act_grad * slope


def pipeline(
    inputs_ref, cot_ref, w_in_ref, w_out_ref, mask_in_ref, mask_out_ref,
    out_ref, ig_ref, xg_out, ahg_out,
    w1, w2, s1, s2, m_in, m_out, a2a_send, a2a_recv, xg, part, rs1_send,
    r1x, r1y, sum_x, sum_y, rs2_sx, rs2_sy, r2y, r2x, ahg, prod, sib_send, sib_recv,
    row_send, row_recv, row_own, hop_send, hop_recv,
    load_sem, wsend_sem, wrecv_sem, a_ssem, a_rsem, g_ssem, g_rsem, f_ssem, f_rsem,
    rs1_ss, rs1_rs, rs2_ss, rs2_rs, ag1_ss, ag1_rs, ag2_ss, ag2_rs,
    sib_ss, sib_rs, row_ss, row_rs, keep_sem, give_ss, give_rs, hop_ss, hop_rs,
):
    row, col = lax.axis_index("row"), lax.axis_index("col")
    z, xh = row // 2, row % 2
    chip, core = col // 2, col % 2
    y, x = chip // 2, chip % 2

    sibling = (row, chip * 2 + 1 - core)
    x_mate = (row, (y * 2 + 1 - x) * 2 + core)
    y_mate = [(row, (flip(y, d) * 2 + x) * 2 + core) for d in (1, 2, 3)]
    hop_mate = (z * 2 + 1 - xh, col)
    z_mate = [(flip(z, d) * 2 + xh, col) for d in (1, 2, 3)]
    col_mate = [(row, (col + d) % 16) for d in range(1, 16)]

    def remote(source, target, send, recv, device):
        return pltpu.make_async_remote_copy(
            src_ref=source, dst_ref=target, send_sem=send, recv_sem=recv,
            device_id=device, device_id_type=MESH,
        )

    loads = [
        pltpu.make_async_copy(w_in_ref.at[:, pl.ds(pl.multiple_of((1 - core) * HALF, HALF), HALF)], s1, load_sem.at[0]),
        pltpu.make_async_copy(w_in_ref.at[:, pl.ds(pl.multiple_of(core * HALF, HALF), HALF)], w1.at[0], load_sem.at[1]),
        pltpu.make_async_copy(w_out_ref.at[pl.ds(pl.multiple_of((1 - core) * HALF, HALF), HALF)], s2, load_sem.at[2]),
        pltpu.make_async_copy(w_out_ref.at[pl.ds(pl.multiple_of(core * HALF, HALF), HALF)], w2.at[0], load_sem.at[3]),
        pltpu.make_async_copy(cot_ref, xg.at[0, 0, 1], load_sem.at[4]),
    ]
    for load in loads:
        load.start()

    barrier = pltpu.get_barrier_semaphore()
    for device in [*col_mate, hop_mate, *z_mate]:
        pl.semaphore_signal(barrier, inc=1, device_id=device, device_id_type=MESH)

    for c in range(16):
        block = inputs_ref[:, c * FEAT : (c + 1) * FEAT].astype(F32)
        a2a_send[c] = jnp.concatenate([block[:, : FEAT // 2], block[:, FEAT // 2 :]], axis=0).astype(BF16)
    pl.semaphore_wait(barrier, 19)

    def a2a_copy(d):
        to = (col + d) % 16
        return remote(a2a_send.at[to], a2a_recv.at[col], a_ssem.at[d - 1], a_rsem.at[d - 1], (row, to))

    for d in range(1, 16):
        a2a_copy(d).start()
    a2a_recv[col] = a2a_send[col]

    mask_in = mask_in_ref[...].astype(F32).astype(BF16)
    m_in[0] = jnp.dot(mask_in, one_hot((48, HALF), 1, 6, core * 24), preferred_element_type=F32)
    m_in[1] = jnp.dot(mask_in, one_hot((48, HALF), 1, 6, (1 - core) * 24), preferred_element_type=F32)
    mask_out = mask_out_ref[...].astype(F32).astype(BF16)
    m_out[...] = jnp.dot(mask_out, one_hot((12, FEAT), 1, 6, 0), preferred_element_type=F32)

    def mask_rows(weight, rows, masks, first):
        def step(i, carry):
            here = pl.ds(pl.multiple_of(i * 64, 64), 64)
            keep = jnp.broadcast_to(masks[pl.ds(first + i, 1), :], (64, masks.shape[1])).astype(BF16)
            weight[here, :] = weight[here, :] * keep
            return carry

        lax.fori_loop(0, rows, step, 0)

    loads[0].wait()
    mask_rows(s1, 12, m_in.at[1], 0)
    give_in = remote(s1, w1.at[1], wsend_sem.at[0], wrecv_sem.at[0], sibling)
    give_in.start()
    loads[1].wait()
    mask_rows(w1.at[0], 12, m_in.at[0], 0)
    loads[2].wait()
    mask_rows(s2, 24, m_out, (1 - core) * 24)
    give_out = remote(s2, w2.at[1], wsend_sem.at[1], wrecv_sem.at[1], sibling)
    give_out.start()
    loads[3].wait()
    mask_rows(w2.at[0], 24, m_out, core * 24)
    loads[4].wait()

    for d in range(1, 16):
        a2a_copy(d).wait_recv()
    for pair in range(8):
        rows = []
        for c in (2 * pair, 2 * pair + 1):
            block = a2a_recv[c].astype(F32)
            rows.append(jnp.concatenate([block[:8], block[8:]], axis=1))
        xg[0, 0, 0, pair * 16 : (pair + 1) * 16, :] = jnp.concatenate(rows, axis=0).astype(BF16)

    def forward(s):
        return remote(xg.at[0, s], xg.at[1, s], f_ssem.at[s], f_rsem.at[s], sibling)

    def group_copy(source, target, device):
        return remote(xg.at[0, source], xg.at[0, target], g_ssem.at[target], g_rsem.at[target], device)

    forward(0).start()
    group_copy(0, 1, hop_mate).start()
    for d in (1, 2, 3):
        group_copy(0, 4 + d, z_mate[d - 1]).start()

    give_in.wait_recv()
    give_out.wait_recv()

    def rs1_copies(s):
        two = s % 2
        far = pl.ds(pl.multiple_of((1 - x) * 64, 64), 64)
        copies = [
            remote(rs1_send.at[two, :, far, 0:XW], r1x.at[s], rs1_ss.at[two, 0], rs1_rs.at[s, 0], x_mate)
        ]
        for d in (1, 2, 3):
            there = pl.ds(pl.multiple_of(flip(y, d) * 32, 32), 32)
            copies.append(
                remote(rs1_send.at[two, :, there, XW:HALF], r1y.at[s, d - 1], rs1_ss.at[two, d], rs1_rs.at[s, d], y_mate[d - 1])
            )
        return copies

    def rs2_copies(s):
        two = s % 2
        far = pl.ds(pl.multiple_of((1 - x) * 16, 16), 16)
        copies = [remote(rs2_sy.at[two, :, far], r2x.at[s], rs2_ss.at[two, 0], rs2_rs.at[s, 0], x_mate)]
        for d in (1, 2, 3):
            there = pl.ds(pl.multiple_of(flip(y, d) * 16, 16), 16)
            copies.append(
                remote(rs2_sx.at[two, :, there], r2y.at[s, d - 1], rs2_ss.at[two, d], rs2_rs.at[s, d], y_mate[d - 1])
            )
        return copies

    def ag1_copies(s):
        two = s % 2
        by_x = ahg.at[s, :, pl.ds(pl.multiple_of(x * 64 + y * 16, 16), 16), 0:XW]
        by_y = ahg.at[s, :, pl.ds(pl.multiple_of(y * 32 + x * 16, 16), 16), XW:HALF]
        copies = [remote(by_y, by_y, ag1_ss.at[two, 0], ag1_rs.at[s, 0], x_mate)]
        for d in (1, 2, 3):
            copies.append(remote(by_x, by_x, ag1_ss.at[two, d], ag1_rs.at[s, d], y_mate[d - 1]))
        return copies

    def ag2_copies(s):
        two = s % 2
        by_x = ahg.at[s, :, pl.ds(pl.multiple_of(x * 64, 64), 64), 0:XW]
        by_y = ahg.at[s, :, pl.ds(pl.multiple_of(y * 32, 32), 32), XW:HALF]
        copies = [remote(by_x, by_x, ag2_ss.at[two, 0], ag2_rs.at[s, 0], x_mate)]
        for d in (1, 2, 3):
            copies.append(remote(by_y, by_y, ag2_ss.at[two, d], ag2_rs.at[s, d], y_mate[d - 1]))
        return copies

    def sib_copy(s):
        two = s % 2
        return remote(sib_send.at[two], sib_recv.at[s], sib_ss.at[two], sib_rs.at[s], sibling)

    def keep_copy(s):
        return pltpu.make_async_copy(ahg.at[s], ahg_out.at[core, s], keep_sem.at[s])

    def give_copy(s):
        return remote(ahg.at[s], ahg_out.at[core, s], give_ss.at[s], give_rs.at[s], sibling)

    def row_copy(s):
        two = s % 2
        by = jnp.where(s < 5, s - 1, s - 4)
        return remote(row_send.at[two], row_recv.at[s], row_ss.at[two], row_rs.at[s], (flip(z, by) * 2 + xh, col))

    def multiply(s):
        two = s % 2
        forward(s).wait_recv()
        for j in range(HALF // TILE):
            here = slice(j * TILE, (j + 1) * TILE)
            total = jnp.dot(xg[0, s, 0], w1[0, :, here], preferred_element_type=F32)
            total += jnp.dot(xg[1, s, 0], w1[1, :, here], preferred_element_type=F32)
            part[two, 0, :, here] = total
            rs1_send[two, 0, :, here] = total.astype(BF16)
        for j in range(HALF // TILE):
            here = slice(j * TILE, (j + 1) * TILE)
            dims = (((1,), (1,)), ((), ()))
            total = lax.dot_general(xg[0, s, 1], w2[0, here, :], dims, preferred_element_type=F32)
            total += lax.dot_general(xg[1, s, 1], w2[1, here, :], dims, preferred_element_type=F32)
            part[two, 1, :, here] = total
            rs1_send[two, 1, :, here] = total.astype(BF16)
        for copy in rs1_copies(s):
            copy.start()

    def receive(s):
        group_copy(0, s, hop_mate).wait_recv()
        forward(s).start()

        @pl.when(s == 1)
        def _():
            for d in (1, 2, 3):
                group_copy(1, 1 + d, z_mate[d - 1]).start()

    def add_first(s):
        two = s % 2
        for copy in rs1_copies(s):
            copy.wait_recv()
        for k in (0, 1):
            total = part[two, k, pl.ds(pl.multiple_of(x * 64, 64), 64), 0:XW] + r1x[s, k].astype(F32)
            sum_x[two, k] = total
            rs2_sx[two, k] = total.astype(BF16)
            total = part[two, k, pl.ds(pl.multiple_of(y * 32, 32), 32), XW:HALF]
            for d in range(3):
                total += r1y[s, d, k].astype(F32)
            sum_y[two, k] = total
            rs2_sy[two, k] = total.astype(BF16)
        for copy in rs2_copies(s):
            copy.start()

    def activate(s):
        two = s % 2
        for copy in rs1_copies(s):
            copy.wait_send()
        for copy in rs2_copies(s):
            copy.wait_recv()
        by_x, by_y = [], []
        for k in (0, 1):
            total = sum_x[two, k, pl.ds(pl.multiple_of(y * 16, 16), 16), :]
            for d in range(3):
                total += r2y[s, d, k].astype(F32)
            by_x.append(total)
            by_y.append(sum_y[two, k, pl.ds(pl.multiple_of(x * 16, 16), 16), :] + r2x[s, k].astype(F32))
        for k, values in enumerate(gelu_parts(*by_x)):
            ahg[s, k, pl.ds(pl.multiple_of(x * 64 + y * 16, 16), 16), 0:XW] = values.astype(BF16)
        for k, values in enumerate(gelu_parts(*by_y)):
            ahg[s, k, pl.ds(pl.multiple_of(y * 32 + x * 16, 16), 16), XW:HALF] = values.astype(BF16)
        for copy in ag1_copies(s):
            copy.start()

    def spread(s):
        for copy in rs2_copies(s):
            copy.wait_send()
        for copy in ag1_copies(s):
            copy.wait_recv()
        for copy in ag2_copies(s):
            copy.start()
        for copy in ag1_copies(s):
            copy.wait_send()

    def project(s):
        two = s % 2
        for copy in ag2_copies(s):
            copy.wait()
        keep_copy(s).start()
        give_copy(s).start()
        for j in range(FEAT // TILE):
            here = slice(j * TILE, (j + 1) * TILE)
            dims = (((1,), (1,)), ((), ()))
            sib_send[two, 0, :, here] = jnp.dot(ahg[s, 0], w2[1, :, here], preferred_element_type=F32).astype(BF16)
            sib_send[two, 1, :, here] = lax.dot_general(
                ahg[s, 1], w1[1, here, :], dims, preferred_element_type=F32
            ).astype(BF16)
        sib_copy(s).start()
        for j in range(FEAT // TILE):
            here = slice(j * TILE, (j + 1) * TILE)
            dims = (((1,), (1,)), ((), ()))
            prod[two, 0, :, here] = jnp.dot(ahg[s, 0], w2[0, :, here], preferred_element_type=F32)
            prod[two, 1, :, here] = lax.dot_general(ahg[s, 1], w1[0, here, :], dims, preferred_element_type=F32)

    def hand_on(s):
        two = s % 2
        sib_copy(s).wait_send()
        sib_copy(s).wait_recv()

        @pl.when(s < 2)
        def _():
            row_own[s] = prod[two] + sib_recv[s].astype(F32)

        @pl.when(s >= 2)
        def _():
            row_send[two] = (prod[two] + sib_recv[s].astype(F32)).astype(BF16)
            row_copy(s).start()

    def finish(s):
        keep_copy(s).wait()
        give_copy(s).wait()

        @pl.when(s >= 2)
        def _():
            row_copy(s).wait_send()

    hop_copy = remote(hop_send, hop_recv, hop_ss, hop_rs, hop_mate)

    def step(t, carry):
        def at(lag, stage):
            pl.when(jnp.logical_and(t >= lag, t < GROUPS + lag))(lambda: stage(t - lag))

        at(6, finish)
        at(3, spread)
        at(2, activate)
        at(1, add_first)
        at(0, multiply)
        pl.when(t < GROUPS - 1)(lambda: receive(t + 1))
        at(4, project)
        at(5, hand_on)

        @pl.when(t == 11)
        def _():
            total = row_own[1]
            for s in (2, 3, 4):
                row_copy(s).wait_recv()
                total += row_recv[s].astype(F32)
            hop_send[...] = total.astype(BF16)
            hop_copy.start()

        return carry

    lax.fori_loop(0, GROUPS + 6, step, 0)

    total = row_own[0]
    for s in (5, 6, 7):
        row_copy(s).wait_recv()
        total += row_recv[s].astype(F32)
    hop_copy.wait()
    total += hop_recv[...].astype(F32)
    out_ref[...] = total[0].astype(BF16)
    ig_ref[...] = total[1].astype(BF16)

    keep_x = pltpu.make_async_copy(xg.at[0], xg_out, load_sem.at[0])
    keep_x.start()
    give_in.wait_send()
    give_out.wait_send()
    for d in range(1, 16):
        a2a_copy(d).wait_send()
    for s in range(GROUPS):
        forward(s).wait_send()
    for s in range(1, GROUPS):
        group_copy(0, s, hop_mate).wait_send()
    keep_x.wait()


def run_pipeline(inputs, cotangent, w_in, w_out, mask_in, mask_out):
    vmem = pl.BlockSpec(memory_space=pltpu.VMEM)
    hbm = pl.BlockSpec(memory_space=pltpu.HBM)
    dma = pltpu.SemaphoreType.DMA
    return pl.pallas_call(
        pipeline,
        out_shape=[
            jax.ShapeDtypeStruct((GROUP, FEAT), BF16),
            jax.ShapeDtypeStruct((GROUP, FEAT), BF16),
            jax.ShapeDtypeStruct((GROUPS, 2, GROUP, FEAT), BF16),
            jax.ShapeDtypeStruct((2, GROUPS, 2, GROUP, HALF), BF16),
        ],
        in_specs=[vmem, hbm, hbm, hbm, vmem, vmem],
        out_specs=[vmem, vmem, hbm, hbm],
        scratch_shapes=[
            pltpu.VMEM((2, FEAT, HALF), BF16),
            pltpu.VMEM((2, HALF, FEAT), BF16),
            pltpu.VMEM((FEAT, HALF), BF16),
            pltpu.VMEM((HALF, FEAT), BF16),
            pltpu.VMEM((2, 12, HALF), F32),
            pltpu.VMEM((48, FEAT), F32),
            pltpu.VMEM((16, 16, FEAT // 2), BF16),
            pltpu.VMEM((16, 16, FEAT // 2), BF16),
            pltpu.VMEM((2, GROUPS, 2, GROUP, FEAT), BF16),
            pltpu.VMEM((2, 2, GROUP, HALF), F32),
            pltpu.VMEM((2, 2, GROUP, HALF), BF16),
            pltpu.VMEM((GROUPS, 2, 64, XW), BF16),
            pltpu.VMEM((GROUPS, 3, 2, 32, YW), BF16),
            pltpu.VMEM((2, 2, 64, XW), F32),
            pltpu.VMEM((2, 2, 32, YW), F32),
            pltpu.VMEM((2, 2, 64, XW), BF16),
            pltpu.VMEM((2, 2, 32, YW), BF16),
            pltpu.VMEM((GROUPS, 3, 2, 16, XW), BF16),
            pltpu.VMEM((GROUPS, 2, 16, YW), BF16),
            pltpu.VMEM((GROUPS, 2, GROUP, HALF), BF16),
            pltpu.VMEM((2, 2, GROUP, FEAT), F32),
            pltpu.VMEM((2, 2, GROUP, FEAT), BF16),
            pltpu.VMEM((GROUPS, 2, GROUP, FEAT), BF16),
            pltpu.VMEM((2, 2, GROUP, FEAT), BF16),
            pltpu.VMEM((GROUPS, 2, GROUP, FEAT), BF16),
            pltpu.VMEM((2, 2, GROUP, FEAT), F32),
            pltpu.VMEM((2, GROUP, FEAT), BF16),
            pltpu.VMEM((2, GROUP, FEAT), BF16),
            dma((5,)), dma((2,)), dma((2,)),
            dma((15,)), dma((15,)),
            dma((GROUPS,)), dma((GROUPS,)), dma((GROUPS,)), dma((GROUPS,)),
            dma((2, 4)), dma((GROUPS, 4)), dma((2, 4)), dma((GROUPS, 4)),
            dma((2, 4)), dma((GROUPS, 4)), dma((2, 4)), dma((GROUPS, 4)),
            dma((2,)), dma((GROUPS,)), dma((2,)), dma((GROUPS,)),
            dma((GROUPS,)), dma((GROUPS,)), dma((GROUPS,)),
            dma, dma,
        ],
        compiler_params=pltpu.CompilerParams(
            collective_id=1, has_side_effects=True, vmem_limit_bytes=60 << 20
        ),
        cost_estimate=pl.CostEstimate(flops=20 << 30, bytes_accessed=30 << 20, transcendentals=1 << 20),
    )(inputs, cotangent, w_in, w_out, mask_in, mask_out)


WIDTH = 512


def weight_grads(x_ref, g_ref, a_ref, h_ref, mask_in_ref, mask_out_ref, w_in_ref, w_out_ref):
    j = pl.program_id(0)
    dims = (((0,), (0,)), ((), ()))
    tokens = GROUP * GROUPS

    mask = mask_in_ref[...].astype(F32).astype(BF16)
    keep = jnp.dot(one_hot((FEAT, 12), 0, 6, 0), mask, preferred_element_type=F32).astype(BF16)
    keep = jnp.dot(keep, one_hot((48, WIDTH), 1, 6, j * (WIDTH // 64)), preferred_element_type=F32)
    product = lax.dot_general(
        x_ref[...].reshape(tokens, FEAT), h_ref[...].reshape(tokens, WIDTH), dims, preferred_element_type=F32
    )
    w_in_ref[...] = (product * keep).astype(BF16)

    mask = mask_out_ref[...].astype(F32).astype(BF16)
    keep = jnp.dot(one_hot((WIDTH, 48), 0, 6, j * (WIDTH // 64)), mask, preferred_element_type=F32).astype(BF16)
    keep = jnp.dot(keep, one_hot((12, FEAT), 1, 6, 0), preferred_element_type=F32)
    product = lax.dot_general(
        a_ref[...].reshape(tokens, WIDTH), g_ref[...].reshape(tokens, FEAT), dims, preferred_element_type=F32
    )
    w_out_ref[...] = (product * keep).astype(BF16)


def run_weight_grads(xg, ahg, mask_in, mask_out):
    per = HALF // WIDTH

    def values(k):
        return pl.BlockSpec((GROUPS, None, GROUP, FEAT), lambda j: (0, k, 0, 0))

    def hidden(k):
        return pl.BlockSpec((None, GROUPS, None, GROUP, WIDTH), lambda j: (j // per, 0, k, 0, j % per))

    return pl.pallas_call(
        weight_grads,
        grid=(2 * per,),
        out_shape=[
            jax.ShapeDtypeStruct((FEAT, 2 * HALF), BF16),
            jax.ShapeDtypeStruct((2 * HALF, FEAT), BF16),
        ],
        in_specs=[
            values(0), values(1), hidden(0), hidden(1),
            pl.BlockSpec((12, 48), lambda j: (0, 0)), pl.BlockSpec((48, 12), lambda j: (0, 0)),
        ],
        out_specs=[pl.BlockSpec((FEAT, WIDTH), lambda j: (0, j)), pl.BlockSpec((WIDTH, FEAT), lambda j: (j, 0))],
        compiler_params=pltpu.CompilerParams(vmem_limit_bytes=48 << 20),
        cost_estimate=pl.CostEstimate(flops=10 << 30, bytes_accessed=25 << 20, transcendentals=0),
    )(xg, xg, ahg, ahg, mask_in, mask_out)


def body(inputs, cotangent, w_in, w_out, mask_in, mask_out):
    output, input_grad, xg, ahg = run_pipeline(inputs, cotangent, w_in, w_out, mask_in, mask_out)
    w_in_grad, w_out_grad = run_weight_grads(xg, ahg, mask_in, mask_out)
    return (output, input_grad, w_in_grad, w_out_grad)


def solution(mesh):
    in_specs = (
        P(("row", "col"), None),
        P("row", "col"),
        P("col", "row"),
        P("row", "col"),
        P("col", "row"),
        P("row", "col"),
    )
    out_specs = (P("row", "col"), P("row", "col"), P("col", "row"), P("row", "col"))
    return jax.shard_map(body, mesh=mesh, in_specs=in_specs, out_specs=out_specs, check_vma=False)
```

time: 661 us -> 197 us (0.30)
  waiting for transfers between devices: 411 us -> 0 us
  Pallas kernels: 0 us -> 189 us
  local copies, waits for them, and re-layouts: 140 us -> 4.64 us
  matrix products: 65.5 us -> 0 us
  other arithmetic: 14.2 us -> 0 us
  between operations: 14.2 us -> 0.67 us
  blocking collectives: 13.1 us -> 0 us
    reduce_scatter x4 -> x0, waiting for transfers between devices: 316 us -> none  [the longest x2 259 us: col_sum(): lax.psum_scatter(product(operand, weight, contract), 'col', scatter_dimen...]
    pallas_call x0 -> x2, Pallas kernels: none -> 189 us  [the longest x1 169 us: run_pipeline(): pl.pallas_call(pipeline, out_shape=[jax.ShapeDtypeStruct((GROUP, FEAT), B...]
    mul x10 -> x0, local copies, waits for them, and re-layouts: 101 us -> none  [masked(): shaped * blocks.astype(weight.dtype)[:, None, :, None]]
    all_gather x4 -> x0, waiting for transfers between devices: 93.5 us -> none  [the longest x2 75.4 us: col_gather(): return lax.all_gather(values, 'col', axis=0, tiled=True)]
    dot_general x6 -> x0, matrix products: 65.5 us -> none  [the longest x4 42.5 us: product(): lax.dot_general(operand, weight, (((1,), (contract,)), ((), ())), preferr...]
    unnamed x12 -> x13, local copies, waits for them, and re-layouts: 39.2 us -> 4.64 us
    all_to_all x1 -> x0, blocking collectives: 13.1 us -> none  [body(): lax.all_to_all(inputs, 'col', split_axis=1, concat_axis=0, tiled=True)]
    mul x1 -> x0, other arithmetic: 7.95 us -> none  [masked(): shaped * blocks.astype(weight.dtype)[:, None, :, None]]
  transfers between devices with their start and end apart: 8 -> 0, of which waited for: 7 -> 0; matrix products, arithmetic and copies ran while one was open for 33% -> 0% of each run, Pallas kernels for 0% -> 0%
where the time goes in v1:
time: 197 us; the launch traced here: 194 us
  Pallas kernels  189 us (96%)
  local copies, waits for them, and re-layouts  4.64 us (2%)
    pallas_call x1, Pallas kernels, run_pipeline(): pl.pallas_call(pipeline, out_shape=[jax.ShapeDtypeStruct((GROUP, FEAT), B...  169 us
    pallas_call x1, Pallas kernels, run_weight_grads(): pl.pallas_call(weight_grads, grid=(2 * per,), out_shape=[jax.ShapeDtypeSt...  19.9 us
    unnamed x13, local copies, waits for them, and re-layouts  4.64 us

profile of v1, /device:TPU:0, one launch (start us, length us, event | category | flops | bytes accessed | tf_op | source)
XLA Modules:
  0.0 194.4 jit_solution(1099008599231204519)
XLA Ops:
  0.6 1.4 copy.10.mask_out_ref
  2.0 0.0 copy-start
  2.0 0.0 copy-start.1
  2.0 169.1 %shard_map.93 = (bf16[128,768]{1,0:T(8,128)(2,1)}, bf16[128,768]{1,0:T(8,128)(2,1)}, bf16[8,2,128,768]{3,2,1,0:T(8,128)(2,1)}, bf16[2,8,2,128,1536]{4,3,2,1,0:T(8,128)(2,1)}) custom-call(bf16[8,12288]{1,0:T(8,128)(2,1)} %inputs_ref.1, bf16[128,768]{1,0:T(8,128)(2,1)} %cot_ref.1, bf16[768,3072]{1,0:T(8,128)(2,1)} %w_in_ref.1, bf16[3072,768]{1,0:T(8,128)(2,1)} %w_out_ref.1, ...), custom_call_target="tpu_custom_call" | custom-call | flops 21474836480 | bytes 31457280 | tf_op jit(solution)/shard_map/pallas_call | solution.py:376
  171.2 0.0 copy-done
  171.2 0.0 copy-done.1
  171.2 0.0 copy-start.2
  171.2 1.9 copy-done.2
  173.1 0.0 copy-start.4
  173.1 0.0 copy-start.3
  173.1 19.9 %shard_map.94 = (bf16[768,3072]{1,0:T(8,128)(2,1)}, bf16[3072,768]{1,0:T(8,128)(2,1)}) custom-call(bf16[8,2,128,768]{3,2,1,0:T(8,128)(2,1)S(1)} %copy-done.2, bf16[8,2,128,768]{3,2,1,0:T(8,128)(2,1)S(1)} %copy-done.2, bf16[2,8,2,128,1536]{4,3,2,1,0:T(8,128)(2,1)} %get-tuple-element.13.a_ref.h_ref, ...), custom_call_target="tpu_custom_call" | custom-call | flops 10737418240 | bytes 26214400 | tf_op jit(solution)/shard_map/pallas_call | solution.py:465
  193.0 0.0 copy-done.4
  193.0 0.7 copy.14
  193.7 0.0 copy-done.3
  193.7 0.7 copy.15
Async XLA Ops:
  2.0 169.2 %copy-start = (s32[48,12]{1,0:T(8,128)S(1)}, s32[48,12]{1,0:T(8,128)}, u32[]{:S(2)}) copy-start(s32[48,12]{1,0:T(8,128)} %copy.10.mask_out_ref) | copy-start | bytes 6916
  2.0 169.2 %copy-start.1 = (s32[12,48]{1,0:T(8,128)S(1)}, s32[12,48]{1,0:T(8,128)}, u32[]{:S(2)}) copy-start(s32[12,48]{1,0:T(8,128)} %mask_in_ref.3) | copy-start | bytes 6916
  171.2 1.9 copy-start.2
  173.1 19.9 %copy-start.4 = (bf16[128,768]{1,0:T(8,128)(2,1)S(1)}, bf16[128,768]{1,0:T(8,128)(2,1)}, u32[]{:S(2)}) copy-start(bf16[128,768]{1,0:T(8,128)(2,1)} %get-tuple-element.20) | copy-start | bytes 589828
  173.1 20.6 %copy-start.3 = (bf16[128,768]{1,0:T(8,128)(2,1)S(1)}, bf16[128,768]{1,0:T(8,128)(2,1)}, u32[]{:S(2)}) copy-start(bf16[128,768]{1,0:T(8,128)(2,1)} %get-tuple-element.21) | copy-start | bytes 589828

commit v2 on v1

v2 whole, which is shorter than its diff:
```python
import functools

import jax
import jax.numpy as jnp
from jax import lax
from jax.experimental import pallas as pl
from jax.experimental.pallas import tpu as pltpu
from jax.sharding import PartitionSpec as P

MESH = pl.DeviceIdType.MESH
F32 = jnp.float32
BF16 = jnp.bfloat16

GROUP = 128
GROUPS = 8
UNITS = 2 * GROUPS
FEAT = 768
COLS = 768
XW = 384
YW = COLS - XW
TILE = 256
NT = (((1,), (1,)), ((), ()))
TN = (((0,), (0,)), ((), ()))


def flip(position, by):
    return (position % 2 + by % 2) % 2 + 2 * ((position // 2 + by // 2) % 2)


def one_hot(shape, along, shift, offset):
    wide = lax.broadcasted_iota(jnp.int32, shape, along)
    other = lax.broadcasted_iota(jnp.int32, shape, 1 - along)
    return (lax.shift_right_logical(wide, shift) + offset == other).astype(F32).astype(BF16)


def gelu_parts(hidden, act_grad):
    c = 0.7978845608028654
    square = hidden * hidden
    inner = jnp.tanh(c * hidden * (1.0 + 0.044715 * square))
    cdf = 0.5 * (1.0 + inner)
    slope = cdf + 0.5 * hidden * (1.0 - inner * inner) * (c * (1.0 + 0.134145 * square))
    return hidden * cdf, act_grad * slope


def pipeline(
    inputs_ref, cot_ref, w_in_ref, w_out_ref, mask_in_ref, mask_out_ref,
    out_ref, ig_ref, xt_out, g_out, at_out, hg_out,
    w1, w2, s1, s2, m_in, m_out, a2a_send, a2a_recv, xg, part, rs1_send,
    r1x, r1y, sum_x, sum_y, rs2_sx, rs2_sy, r2y, r2x, ahg, prod, sib_send, sib_recv,
    row_send, row_recv, row_own, hop_send, hop_recv, at_buf, xt_buf,
    load_sem, wsend_sem, wrecv_sem, a_ssem, a_rsem, g_ssem, g_rsem, f_ssem, f_rsem,
    rs1_ss, rs1_rs, rs2_ss, rs2_rs, ag1_ss, ag1_rs, ag2_ss, ag2_rs,
    sib_ss, sib_rs, row_ss, row_rs, keep_sem, give_ss, give_rs, store_sem, hop_ss, hop_rs,
):
    row, col = lax.axis_index("row"), lax.axis_index("col")
    z, xh = row // 2, row % 2
    chip, core = col // 2, col % 2
    y, x = chip // 2, chip % 2

    sibling = (row, chip * 2 + 1 - core)
    x_mate = (row, (y * 2 + 1 - x) * 2 + core)
    y_mate = [(row, (flip(y, d) * 2 + x) * 2 + core) for d in (1, 2, 3)]
    hop_mate = (z * 2 + 1 - xh, col)
    z_mate = [(flip(z, d) * 2 + xh, col) for d in (1, 2, 3)]
    col_mate = [(row, (col + d) % 16) for d in range(1, 16)]

    def remote(source, target, send, recv, device):
        return pltpu.make_async_remote_copy(
            src_ref=source, dst_ref=target, send_sem=send, recv_sem=recv,
            device_id=device, device_id_type=MESH,
        )

    def part_of(base, u):
        return pl.ds(pl.multiple_of(base * 2 * COLS + u * COLS, COLS), COLS)

    loads = []
    for u in (0, 1):
        loads += [
            (w_out_ref.at[part_of(1 - core, u), :], s2.at[u]),
            (w_in_ref.at[:, part_of(1 - core, u)], s1.at[u]),
            (w_out_ref.at[part_of(core, u), :], w2.at[0, u]),
            (w_in_ref.at[:, part_of(core, u)], w1.at[0, u]),
        ]
    loads.append((cot_ref, xg.at[0, GROUPS - 1, 1]))
    loads = [pltpu.make_async_copy(*pair, load_sem.at[i]) for i, pair in enumerate(loads)]
    for load in loads:
        load.start()

    barrier = pltpu.get_barrier_semaphore()
    for device in [*col_mate, hop_mate, *z_mate]:
        pl.semaphore_signal(barrier, inc=1, device_id=device, device_id_type=MESH)

    for c in range(16):
        block = inputs_ref[:, c * FEAT : (c + 1) * FEAT].astype(F32)
        a2a_send[c] = jnp.concatenate([block[:, : FEAT // 2], block[:, FEAT // 2 :]], axis=0).astype(BF16)
    pl.semaphore_wait(barrier, 19)

    def a2a_copy(d):
        to = (col + d) % 16
        return remote(a2a_send.at[to], a2a_recv.at[col], a_ssem.at[d - 1], a_rsem.at[d - 1], (row, to))

    for d in range(1, 16):
        a2a_copy(d).start()
    a2a_recv[col] = a2a_send[col]

    def group_copy(source, target, k, device):
        return remote(xg.at[0, source, k], xg.at[0, target, k], g_ssem.at[target, k], g_rsem.at[target, k], device)

    def forward(s):
        return remote(xg.at[0, s], xg.at[1, s], f_ssem.at[s], f_rsem.at[s], sibling)

    mask_in = mask_in_ref[...].astype(F32).astype(BF16)
    m_in[0] = jnp.dot(mask_in, one_hot((48, 2 * COLS), 1, 6, core * 24), preferred_element_type=F32)
    m_in[1] = jnp.dot(mask_in, one_hot((48, 2 * COLS), 1, 6, (1 - core) * 24), preferred_element_type=F32)
    mask_out = mask_out_ref[...].astype(F32).astype(BF16)
    m_out[...] = lax.dot_general(mask_out, one_hot((12, FEAT), 1, 6, 0), TN, preferred_element_type=F32)

    def mask_rows(weight, masks, first, columns):
        def step(i, carry):
            here = pl.ds(pl.multiple_of(i * 64, 64), 64)
            keep = jnp.broadcast_to(masks[pl.ds(first + i, 1), columns], (64, COLS)).astype(BF16)
            weight[here, :] = weight[here, :] * keep
            return carry

        lax.fori_loop(0, 12, step, 0)

    gives = []
    loads[8].wait()
    group_copy(7, 0, 1, z_mate[0]).start()
    group_copy(7, 1, 1, hop_mate).start()
    for u in (0, 1):
        columns = slice(u * COLS, (u + 1) * COLS)
        loads[4 * u].wait()
        mask_rows(s2.at[u], m_out, (1 - core) * 24 + u * 12, slice(None))
        gives.append(remote(s2.at[u], w2.at[1, u], wsend_sem.at[2 * u], wrecv_sem.at[2 * u], sibling))
        gives[-1].start()
        loads[4 * u + 1].wait()
        mask_rows(s1.at[u], m_in.at[1], 0, columns)
        gives.append(remote(s1.at[u], w1.at[1, u], wsend_sem.at[2 * u + 1], wrecv_sem.at[2 * u + 1], sibling))
        gives[-1].start()

    for d in range(1, 16):
        a2a_copy(d).wait_recv()
    for pair in range(8):
        rows = []
        for c in (2 * pair, 2 * pair + 1):
            block = a2a_recv[c].astype(F32)
            rows.append(jnp.concatenate([block[:8], block[8:]], axis=1))
        xg[0, 7, 0, pair * 16 : (pair + 1) * 16, :] = jnp.concatenate(rows, axis=0).astype(BF16)
    group_copy(7, 0, 0, z_mate[0]).start()
    group_copy(7, 1, 0, hop_mate).start()

    for u in (0, 1):
        loads[4 * u + 2].wait()
        mask_rows(w2.at[0, u], m_out, core * 24 + u * 12, slice(None))
        loads[4 * u + 3].wait()
        mask_rows(w1.at[0, u], m_in.at[0], 0, slice(u * COLS, (u + 1) * COLS))

    for k in (0, 1):
        group_copy(7, 0, k, z_mate[0]).wait_recv()
    forward(0).start()
    for give in gives:
        give.wait_recv()

    def rs1_copies(n):
        two = n % 2
        far = pl.ds(pl.multiple_of((1 - x) * 64, 64), 64)
        copies = [remote(rs1_send.at[two, :, far, 0:XW], r1x.at[n], rs1_ss.at[two, 0], rs1_rs.at[n, 0], x_mate)]
        for d in (1, 2, 3):
            there = pl.ds(pl.multiple_of(flip(y, d) * 32, 32), 32)
            copies.append(
                remote(rs1_send.at[two, :, there, XW:COLS], r1y.at[n, d - 1], rs1_ss.at[two, d], rs1_rs.at[n, d], y_mate[d - 1])
            )
        return copies

    def rs2_copies(n):
        two = n % 2
        far = pl.ds(pl.multiple_of((1 - x) * 16, 16), 16)
        copies = [remote(rs2_sy.at[two, :, far], r2x.at[n], rs2_ss.at[two, 0], rs2_rs.at[n, 0], x_mate)]
        for d in (1, 2, 3):
            there = pl.ds(pl.multiple_of(flip(y, d) * 16, 16), 16)
            copies.append(
                remote(rs2_sx.at[two, :, there], r2y.at[n, d - 1], rs2_ss.at[two, d], rs2_rs.at[n, d], y_mate[d - 1])
            )
        return copies

    def ag1_copies(n):
        two = n % 2
        by_x = ahg.at[n, :, pl.ds(pl.multiple_of(x * 64 + y * 16, 16), 16), 0:XW]
        by_y = ahg.at[n, :, pl.ds(pl.multiple_of(y * 32 + x * 16, 16), 16), XW:COLS]
        copies = [remote(by_y, by_y, ag1_ss.at[two, 0], ag1_rs.at[n, 0], x_mate)]
        for d in (1, 2, 3):
            copies.append(remote(by_x, by_x, ag1_ss.at[two, d], ag1_rs.at[n, d], y_mate[d - 1]))
        return copies

    def ag2_copies(n):
        two = n % 2
        by_x = ahg.at[n, :, pl.ds(pl.multiple_of(x * 64, 64), 64), 0:XW]
        by_y = ahg.at[n, :, pl.ds(pl.multiple_of(y * 32, 32), 32), XW:COLS]
        copies = [remote(by_x, by_x, ag2_ss.at[two, 0], ag2_rs.at[n, 0], x_mate)]
        for d in (1, 2, 3):
            copies.append(remote(by_y, by_y, ag2_ss.at[two, d], ag2_rs.at[n, d], y_mate[d - 1]))
        return copies

    def sib_copy(s):
        two = s % 2
        return remote(sib_send.at[two], sib_recv.at[s], sib_ss.at[two], sib_rs.at[s], sibling)

    def tokens_of(s):
        return pl.ds(pl.multiple_of(s * GROUP, GROUP), GROUP)

    def keep_copies(n):
        s, u, two = n // 2, n % 2, n % 2
        pairs = [(at_buf.at[two], at_out.at[core, u, :, tokens_of(s)]), (ahg.at[n, 1], hg_out.at[core, u, tokens_of(s), :])]
        copies = []
        for k, (source, target) in enumerate(pairs):
            copies.append(pltpu.make_async_copy(source, target, keep_sem.at[two, k]))
            copies.append(remote(source, target, give_ss.at[two, k], give_rs.at[n, k], sibling))
        return copies

    def store_copies(s):
        return [
            pltpu.make_async_copy(xt_buf, xt_out.at[:, tokens_of(s)], store_sem.at[0]),
            pltpu.make_async_copy(xg.at[0, s, 1], g_out.at[tokens_of(s), :], store_sem.at[1]),
        ]

    def row_copy(s):
        two = s % 2
        by = jnp.where(s == 0, 1, jnp.where(s < 5, s - 1, s - 3))
        return remote(row_send.at[two], row_recv.at[s], row_ss.at[two], row_rs.at[s], (flip(z, by) * 2 + xh, col))

    def multiply(n):
        s, u, two = n // 2, n % 2, n % 2

        @pl.when(u == 0)
        def _():
            forward(s).wait_recv()

        for j in range(COLS // TILE):
            here = slice(j * TILE, (j + 1) * TILE)
            total = lax.dot_general(xg[0, s, 1], w2[0, u, here, :], NT, preferred_element_type=F32)
            total += lax.dot_general(xg[1, s, 1], w2[1, u, here, :], NT, preferred_element_type=F32)
            part[two, 1, :, here] = total
            rs1_send[two, 1, :, here] = total.astype(BF16)
        for j in range(COLS // TILE):
            here = slice(j * TILE, (j + 1) * TILE)
            total = jnp.dot(xg[0, s, 0], w1[0, u, :, here], preferred_element_type=F32)
            total += jnp.dot(xg[1, s, 0], w1[1, u, :, here], preferred_element_type=F32)
            part[two, 0, :, here] = total
            rs1_send[two, 0, :, here] = total.astype(BF16)
        for copy in rs1_copies(n):
            copy.start()

    def receive(s):
        @pl.when(s < GROUPS - 1)
        def _():
            for k in (0, 1):
                group_copy(7, s, k, hop_mate).wait_recv()

        forward(s).start()
        for at, source, target, d in ((1, 1, 2, 1), (2, 1, 3, 2), (2, 1, 4, 3), (3, 7, 5, 2), (3, 7, 6, 3)):

            @pl.when(s == at)
            def _(source=source, target=target, d=d):
                for k in (0, 1):
                    group_copy(source, target, k, z_mate[d - 1]).start()

    def add_first(n):
        two = n % 2
        for copy in rs1_copies(n):
            copy.wait()
        for k in (0, 1):
            total = part[two, k, pl.ds(pl.multiple_of(x * 64, 64), 64), 0:XW] + r1x[n, k].astype(F32)
            sum_x[two, k] = total
            rs2_sx[two, k] = total.astype(BF16)
            total = part[two, k, pl.ds(pl.multiple_of(y * 32, 32), 32), XW:COLS]
            for d in range(3):
                total += r1y[n, d, k].astype(F32)
            sum_y[two, k] = total
            rs2_sy[two, k] = total.astype(BF16)
        for copy in rs2_copies(n):
            copy.start()

    def activate(n):
        two = n % 2
        for copy in rs2_copies(n):
            copy.wait()
        by_x, by_y = [], []
        for k in (0, 1):
            total = sum_x[two, k, pl.ds(pl.multiple_of(y * 16, 16), 16), :]
            for d in range(3):
                total += r2y[n, d, k].astype(F32)
            by_x.append(total)
            by_y.append(sum_y[two, k, pl.ds(pl.multiple_of(x * 16, 16), 16), :] + r2x[n, k].astype(F32))
        for k, values in enumerate(gelu_parts(*by_x)):
            ahg[n, k, pl.ds(pl.multiple_of(x * 64 + y * 16, 16), 16), 0:XW] = values.astype(BF16)
        for k, values in enumerate(gelu_parts(*by_y)):
            ahg[n, k, pl.ds(pl.multiple_of(y * 32 + x * 16, 16), 16), XW:COLS] = values.astype(BF16)
        for copy in ag1_copies(n):
            copy.start()

    def spread(n):
        for copy in ag1_copies(n):
            copy.wait()
        for copy in ag2_copies(n):
            copy.start()

    def project(n):
        s, u, two = n // 2, n % 2, (n // 2) % 2
        for copy in ag2_copies(n):
            copy.wait()

        def products(fc, here):
            return (
                jnp.dot(ahg[n, 0], w2[fc, u, :, here], preferred_element_type=F32),
                lax.dot_general(ahg[n, 1], w1[fc, u, here, :], NT, preferred_element_type=F32),
            )

        @pl.when(u == 0)
        def _():
            for fc in (1, 0):
                for j in range(FEAT // TILE):
                    here = slice(j * TILE, (j + 1) * TILE)
                    for k, value in enumerate(products(fc, here)):
                        prod[two, fc, k, :, here] = value

        @pl.when(u == 1)
        def _():
            for j in range(FEAT // TILE):
                here = slice(j * TILE, (j + 1) * TILE)
                for k, value in enumerate(products(1, here)):
                    sib_send[two, k, :, here] = (prod[two, 1, k, :, here] + value).astype(BF16)
            sib_copy(s).start()
            for j in range(FEAT // TILE):
                here = slice(j * TILE, (j + 1) * TILE)
                for k, value in enumerate(products(0, here)):
                    prod[two, 0, k, :, here] += value

        at_buf[n % 2] = ahg[n, 0].T
        for copy in keep_copies(n):
            copy.start()

        @pl.when(u == 0)
        def _():
            xt_buf[...] = xg[0, s, 0].T
            for copy in store_copies(s):
                copy.start()

    def hand_on(n):
        s, two = n // 2, (n // 2) % 2

        @pl.when(n % 2 == 1)
        def _():
            sib_copy(s).wait()

            @pl.when(jnp.logical_or(s == 1, s == 7))
            def _():
                row_own[jnp.where(s == 1, 1, 0)] = prod[two, 0] + sib_recv[s].astype(F32)

            @pl.when(jnp.logical_and(s != 1, s != 7))
            def _():
                row_send[two] = (prod[two, 0] + sib_recv[s].astype(F32)).astype(BF16)
                row_copy(s).start()

    def finish(n):
        s = n // 2
        for copy in keep_copies(n):
            copy.wait()

        @pl.when(n % 2 == 0)
        def _():
            for copy in store_copies(s):
                copy.wait()

    def settle(n):
        s = n // 2

        @pl.when(jnp.logical_and(n % 2 == 1, jnp.logical_and(s != 1, s != 7)))
        def _():
            row_copy(s).wait_send()

    hop_copy = remote(hop_send, hop_recv, hop_ss, hop_rs, hop_mate)

    def step(t, carry):
        def at(lag, stage):
            pl.when(jnp.logical_and(t >= lag, t < UNITS + lag))(lambda: stage(t - lag))

        at(0, multiply)
        at(1, add_first)
        at(2, activate)
        at(3, spread)

        @pl.when(jnp.logical_and(t % 2 == 0, t < UNITS - 2))
        def _():
            receive(t // 2 + 1)

        at(5, finish)
        at(4, project)
        at(7, settle)
        at(5, hand_on)

        @pl.when(t == 16)
        def _():
            total = row_own[1]
            for s in (2, 3, 4):
                row_copy(s).wait_recv()
                total += row_recv[s].astype(F32)
            hop_send[...] = total.astype(BF16)
            hop_copy.start()

        return carry

    lax.fori_loop(0, UNITS + 5, step, 0)

    total = row_own[0]
    for s in (0, 5, 6):
        row_copy(s).wait_recv()
        total += row_recv[s].astype(F32)
    hop_copy.wait()
    total += hop_recv[...].astype(F32)
    out_ref[...] = total[0].astype(BF16)
    ig_ref[...] = total[1].astype(BF16)

    for give in gives:
        give.wait_send()
    for d in range(1, 16):
        a2a_copy(d).wait_send()
    for s in range(GROUPS):
        forward(s).wait_send()
    for s in range(GROUPS - 1):
        for k in (0, 1):
            group_copy(7, s, k, hop_mate).wait_send()


def run_pipeline(inputs, cotangent, w_in, w_out, mask_in, mask_out):
    vmem = pl.BlockSpec(memory_space=pltpu.VMEM)
    hbm = pl.BlockSpec(memory_space=pltpu.HBM)
    dma = pltpu.SemaphoreType.DMA
    tokens = GROUP * GROUPS
    return pl.pallas_call(
        pipeline,
        out_shape=[
            jax.ShapeDtypeStruct((GROUP, FEAT), BF16),
            jax.ShapeDtypeStruct((GROUP, FEAT), BF16),
            jax.ShapeDtypeStruct((FEAT, tokens), BF16),
            jax.ShapeDtypeStruct((tokens, FEAT), BF16),
            jax.ShapeDtypeStruct((2, 2, COLS, tokens), BF16),
            jax.ShapeDtypeStruct((2, 2, tokens, COLS), BF16),
        ],
        in_specs=[vmem, hbm, hbm, hbm, vmem, vmem],
        out_specs=[vmem, vmem, hbm, hbm, hbm, hbm],
        scratch_shapes=[
            pltpu.VMEM((2, 2, FEAT, COLS), BF16),
            pltpu.VMEM((2, 2, COLS, FEAT), BF16),
            pltpu.VMEM((2, FEAT, COLS), BF16),
            pltpu.VMEM((2, COLS, FEAT), BF16),
            pltpu.VMEM((2, 12, 2 * COLS), F32),
            pltpu.VMEM((48, FEAT), F32),
            pltpu.VMEM((16, 16, FEAT // 2), BF16),
            pltpu.VMEM((16, 16, FEAT // 2), BF16),
            pltpu.VMEM((2, GROUPS, 2, GROUP, FEAT), BF16),
            pltpu.VMEM((2, 2, GROUP, COLS), F32),
            pltpu.VMEM((2, 2, GROUP, COLS), BF16),
            pltpu.VMEM((UNITS, 2, 64, XW), BF16),
            pltpu.VMEM((UNITS, 3, 2, 32, YW), BF16),
            pltpu.VMEM((2, 2, 64, XW), F32),
            pltpu.VMEM((2, 2, 32, YW), F32),
            pltpu.VMEM((2, 2, 64, XW), BF16),
            pltpu.VMEM((2, 2, 32, YW), BF16),
            pltpu.VMEM((UNITS, 3, 2, 16, XW), BF16),
            pltpu.VMEM((UNITS, 2, 16, YW), BF16),
            pltpu.VMEM((UNITS, 2, GROUP, COLS), BF16),
            pltpu.VMEM((2, 2, 2, GROUP, FEAT), F32),
            pltpu.VMEM((2, 2, GROUP, FEAT), BF16),
            pltpu.VMEM((GROUPS, 2, GROUP, FEAT), BF16),
            pltpu.VMEM((2, 2, GROUP, FEAT), BF16),
            pltpu.VMEM((GROUPS, 2, GROUP, FEAT), BF16),
            pltpu.VMEM((2, 2, GROUP, FEAT), F32),
            pltpu.VMEM((2, GROUP, FEAT), BF16),
            pltpu.VMEM((2, GROUP, FEAT), BF16),
            pltpu.VMEM((2, COLS, GROUP), BF16),
            pltpu.VMEM((FEAT, GROUP), BF16),
            dma((9,)), dma((4,)), dma((4,)),
            dma((15,)), dma((15,)),
            dma((GROUPS, 2)), dma((GROUPS, 2)), dma((GROUPS,)), dma((GROUPS,)),
            dma((2, 4)), dma((UNITS, 4)), dma((2, 4)), dma((UNITS, 4)),
            dma((2, 4)), dma((UNITS, 4)), dma((2, 4)), dma((UNITS, 4)),
            dma((2,)), dma((GROUPS,)), dma((2,)), dma((GROUPS,)),
            dma((2, 2)), dma((2, 2)), dma((UNITS, 2)), dma((2,)),
            dma, dma,
        ],
        compiler_params=pltpu.CompilerParams(
            collective_id=1, has_side_effects=True, vmem_limit_bytes=60 << 20
        ),
        cost_estimate=pl.CostEstimate(flops=20 << 30, bytes_accessed=30 << 20, transcendentals=1 << 20),
    )(inputs, cotangent, w_in, w_out, mask_in, mask_out)


def weight_grads(
    xt_ref, g_ref, at_ref, hg_ref, mask_in_ref, mask_out_ref, out_in, ig_in, w_in_ref, w_out_ref, out_ref, ig_ref
):
    j = pl.program_id(0)

    @pl.when(j == 0)
    def _():
        out_ref[...] = out_in[...]
        ig_ref[...] = ig_in[...]

    mask = mask_in_ref[...].astype(F32).astype(BF16)
    keep = jnp.dot(one_hot((FEAT, 12), 0, 6, 0), mask, preferred_element_type=F32).astype(BF16)
    keep = jnp.dot(keep, one_hot((48, COLS), 1, 6, j * (COLS // 64)), preferred_element_type=F32)
    w_in_ref[...] = (jnp.dot(xt_ref[...], hg_ref[...], preferred_element_type=F32) * keep).astype(BF16)

    mask = mask_out_ref[...].astype(F32).astype(BF16)
    keep = lax.dot_general(one_hot((COLS, 48), 0, 6, j * (COLS // 64)), mask, NT, preferred_element_type=F32).astype(BF16)
    keep = jnp.dot(keep, one_hot((12, FEAT), 1, 6, 0), preferred_element_type=F32)
    w_out_ref[...] = (jnp.dot(at_ref[...], g_ref[...], preferred_element_type=F32) * keep).astype(BF16)


def run_weight_grads(output, input_grad, xt, g, at, hg, mask_in, mask_out):
    tokens = GROUP * GROUPS

    def whole(*shape):
        return pl.BlockSpec(shape, lambda j: (0, 0))

    def tile(*shape):
        return pl.BlockSpec((None, None, *shape), lambda j: (j // 2, j % 2, 0, 0))

    return pl.pallas_call(
        weight_grads,
        grid=(4,),
        out_shape=[
            jax.ShapeDtypeStruct((FEAT, 4 * COLS), BF16),
            jax.ShapeDtypeStruct((4 * COLS, FEAT), BF16),
            jax.ShapeDtypeStruct((GROUP, FEAT), BF16),
            jax.ShapeDtypeStruct((GROUP, FEAT), BF16),
        ],
        in_specs=[
            whole(FEAT, tokens), whole(tokens, FEAT), tile(COLS, tokens), tile(tokens, COLS),
            whole(12, 48), whole(12, 48), whole(GROUP, FEAT), whole(GROUP, FEAT),
        ],
        out_specs=[
            pl.BlockSpec((FEAT, COLS), lambda j: (0, j)), pl.BlockSpec((COLS, FEAT), lambda j: (j, 0)),
            whole(GROUP, FEAT), whole(GROUP, FEAT),
        ],
        compiler_params=pltpu.CompilerParams(vmem_limit_bytes=60 << 20),
        cost_estimate=pl.CostEstimate(flops=10 << 30, bytes_accessed=25 << 20, transcendentals=0),
    )(xt, g, at, hg, mask_in, mask_out, output, input_grad)


def body(inputs, cotangent, w_in, w_out, mask_in, mask_out):
    mask_out = mask_out.T
    made = run_pipeline(inputs, cotangent, w_in, w_out, mask_in, mask_out)
    w_in_grad, w_out_grad, output, input_grad = run_weight_grads(*made, mask_in, mask_out)
    return (output, input_grad, w_in_grad, w_out_grad)


def solution(mesh):
    in_specs = (
        P(("row", "col"), None),
        P("row", "col"),
        P("col", "row"),
        P("row", "col"),
        P("col", "row"),
        P("row", "col"),
    )
    out_specs = (P("row", "col"), P("row", "col"), P("col", "row"), P("row", "col"))
    return jax.shard_map(body, mesh=mesh, in_specs=in_specs, out_specs=out_specs, check_vma=False)
```

time: 197 us -> 170 us (0.86)
  Pallas kernels: 189 us -> 168 us
  local copies, waits for them, and re-layouts: 4.64 us -> 0 us
    pallas_call x1, Pallas kernels: 169 us -> 150 us  [run_pipeline(): pl.pallas_call(pipeline, out_shape=[jax.ShapeDtypeStruct((GROUP, FEAT), B...]
    unnamed x13 -> x0, local copies, waits for them, and re-layouts: 4.64 us -> none
    pallas_call x1, Pallas kernels: 19.9 us -> 17.8 us  [run_weight_grads(): pl.pallas_call(weight_grads, grid=(4,), out_shape=[jax.ShapeDtypeStruct((...]
where the time goes in v2:
time: 170 us; the launch traced here: 169 us
  Pallas kernels  168 us (99%)
    pallas_call x1, Pallas kernels, run_pipeline(): pl.pallas_call(pipeline, out_shape=[jax.ShapeDtypeStruct((GROUP, FEAT), B...  150 us
    pallas_call x1, Pallas kernels, run_weight_grads(): pl.pallas_call(weight_grads, grid=(4,), out_shape=[jax.ShapeDtypeStruct((...  17.8 us

profile of v2, /device:TPU:0, one launch (start us, length us, event | category | flops | bytes accessed | tf_op | source)
XLA Modules:
  0.0 168.5 jit_solution(2779302189694263031)
XLA Ops:
  0.6 150.0 %shard_map.93 = (bf16[128,768]{1,0:T(8,128)(2,1)}, bf16[128,768]{1,0:T(8,128)(2,1)}, bf16[768,1024]{1,0:T(8,128)(2,1)}, bf16[1024,768]{1,0:T(8,128)(2,1)}, bf16[...) custom-call(bf16[8,12288]{1,0:T(8,128)(2,1)} %inputs_ref.1, bf16[128,768]{1,0:T(8,128)(2,1)} %cot_ref.1, ...), custom_call_target="tpu_custom_call" | custom-call | flops 21474836480 | bytes 31457280 | tf_op jit(solution)/shard_map/pallas_call | solution.py:440
  150.7 17.8 %shard_map.94 = (bf16[768,3072]{1,0:T(8,128)(2,1)}, bf16[3072,768]{1,0:T(8,128)(2,1)}, bf16[128,768]{1,0:T(8,128)(2,1)}, bf16[128,768]{1,0:T(8,128)(2,1)}) custom-call(bf16[768,1024]{1,0:T(8,128)(2,1)} %get-tuple-element.14.xt_ref, bf16[1024,768]{1,0:T(8,128)(2,1)} %get-tuple-element.15.g_ref, bf16[2,2,768,1024]{3,2,1,0:T(8,128)(2,1)} %get-tuple-element.16.at_ref, ...), custom_call_target="tpu_custom_call" | custom-call | flops 10737418240 | bytes 26214400 | tf_op jit(solution)/shard_map/pallas_call | solution.py:529

commit v3 on v2

v3 whole, which is shorter than its diff:
```python
import functools

import jax
import jax.numpy as jnp
from jax import lax
from jax.experimental import pallas as pl
from jax.experimental.pallas import tpu as pltpu
from jax.sharding import PartitionSpec as P

MESH = pl.DeviceIdType.MESH
F32 = jnp.float32
BF16 = jnp.bfloat16

GROUP = 128
GROUPS = 8
UNITS = 2 * GROUPS
FEAT = 768
COLS = 768
RANGES = (((0, 128), (0, 1, 2)), ((128, 256), (0, 2, 1)), ((256, 512), (1, 2, 0)), ((512, 768), (2, 1, 0)))
TILE = 256
NT = (((1,), (1,)), ((), ()))
TN = (((0,), (0,)), ((), ()))


def flip(position, by):
    return (position % 2 + by % 2) % 2 + 2 * ((position // 2 + by // 2) % 2)


def one_hot(shape, along, shift, offset):
    wide = lax.broadcasted_iota(jnp.int32, shape, along)
    other = lax.broadcasted_iota(jnp.int32, shape, 1 - along)
    return (lax.shift_right_logical(wide, shift) + offset == other).astype(F32).astype(BF16)


def gelu_parts(hidden, act_grad):
    c = 0.7978845608028654
    square = hidden * hidden
    inner = jnp.tanh(c * hidden * (1.0 + 0.044715 * square))
    cdf = 0.5 * (1.0 + inner)
    slope = cdf + 0.5 * hidden * (1.0 - inner * inner) * (c * (1.0 + 0.134145 * square))
    return hidden * cdf, act_grad * slope


def pipeline(
    inputs_ref, cot_ref, w_in_ref, w_out_ref, mask_in_ref, mask_out_ref,
    out_ref, ig_ref, xt_out, g_out, at_out, hg_out,
    w1, w2, s1, s2, m_in, m_out, a2a_send, a2a_recv, xg, part, part_send,
    half, half_send, quarter, quarter_send, half_recv, quarter_recv, eighth_recv, ahg, prod, sib_send, sib_recv,
    row_send, row_recv, row_own, hop_send, hop_recv, at_buf, hg_buf, xt_buf,
    load_sem, wsend_sem, wrecv_sem, a_ssem, a_rsem, g_ssem, g_rsem, f_ssem, f_rsem,
    sum_ss, sum_rs, gather_ss, gather_rs,
    sib_ss, sib_rs, row_ss, row_rs, keep_sem, give_ss, give_rs, store_sem, hop_ss, hop_rs,
):
    row, col = lax.axis_index("row"), lax.axis_index("col")
    z, xh = row // 2, row % 2
    chip, core = col // 2, col % 2
    y, x = chip // 2, chip % 2

    sibling = (row, chip * 2 + 1 - core)
    x_mate = (row, (y * 2 + 1 - x) * 2 + core)
    mate = [x_mate] + [(row, (flip(y, d) * 2 + x) * 2 + core) for d in (1, 3)]
    bit = [x, (y // 2 + y % 2) % 2, y // 2]
    hop_mate = (z * 2 + 1 - xh, col)
    z_mate = [(flip(z, d) * 2 + xh, col) for d in (1, 2, 3)]
    col_mate = [(row, (col + d) % 16) for d in range(1, 16)]
    near = z * 2 + 1 - xh
    near_mate = [(near, (col + d) % 16) for d in range(1, 16)]

    def remote(source, target, send, recv, device):
        return pltpu.make_async_remote_copy(
            src_ref=source, dst_ref=target, send_sem=send, recv_sem=recv,
            device_id=device, device_id_type=MESH,
        )

    def part_of(base, u):
        return pl.ds(pl.multiple_of(base * 2 * COLS + u * COLS, COLS), COLS)

    loads = []
    for u in (0, 1):
        loads += [
            (w_out_ref.at[part_of(1 - core, u), :], s2.at[u]),
            (w_in_ref.at[:, part_of(1 - core, u)], s1.at[u]),
            (w_out_ref.at[part_of(core, u), :], w2.at[0, u]),
            (w_in_ref.at[:, part_of(core, u)], w1.at[0, u]),
        ]
    loads.append((cot_ref, xg.at[0, GROUPS - 1, 1]))
    loads = [pltpu.make_async_copy(*pair, load_sem.at[i]) for i, pair in enumerate(loads)]
    for load in loads:
        load.start()

    barrier = pltpu.get_barrier_semaphore()
    for device in [*col_mate, *near_mate, hop_mate, *z_mate]:
        pl.semaphore_signal(barrier, inc=1, device_id=device, device_id_type=MESH)

    for c in range(16):
        block = inputs_ref[:, c * FEAT : (c + 1) * FEAT].astype(F32)
        a2a_send[c] = jnp.concatenate([block[:, : FEAT // 2], block[:, FEAT // 2 :]], axis=0).astype(BF16)
    pl.semaphore_wait(barrier, 34)

    def a2a_copy(d, other):
        to = (col + d) % 16
        device = (near if other else row, to)
        return remote(a2a_send.at[to], a2a_recv.at[other, col], a_ssem.at[other, d], a_rsem.at[other, d], device)

    a2a_copies = [a2a_copy(d, 1) for d in range(16)] + [a2a_copy(d, 0) for d in range(1, 16)]
    for copy in a2a_copies:
        copy.start()
    a2a_recv[0, col] = a2a_send[col]

    def group_copy(source, target, k, device):
        return remote(xg.at[0, source, k], xg.at[0, target, k], g_ssem.at[target, k], g_rsem.at[target, k], device)

    def forward(s):
        return remote(xg.at[0, s], xg.at[1, s], f_ssem.at[s], f_rsem.at[s], sibling)

    mask_in = mask_in_ref[...].astype(F32).astype(BF16)
    m_in[0] = jnp.dot(mask_in, one_hot((48, 2 * COLS), 1, 6, core * 24), preferred_element_type=F32)
    m_in[1] = jnp.dot(mask_in, one_hot((48, 2 * COLS), 1, 6, (1 - core) * 24), preferred_element_type=F32)
    mask_out = mask_out_ref[...].astype(F32).astype(BF16)
    m_out[...] = lax.dot_general(mask_out, one_hot((12, FEAT), 1, 6, 0), TN, preferred_element_type=F32)

    def mask_rows(weight, masks, first, columns):
        def step(i, carry):
            here = pl.ds(pl.multiple_of(i * 64, 64), 64)
            keep = jnp.broadcast_to(masks[pl.ds(first + i, 1), columns], (64, COLS)).astype(BF16)
            weight[here, :] = weight[here, :] * keep
            return carry

        lax.fori_loop(0, 12, step, 0)

    gives = []
    loads[8].wait()
    group_copy(7, 0, 1, hop_mate).start()
    for u in (0, 1):
        columns = slice(u * COLS, (u + 1) * COLS)
        loads[4 * u].wait()
        mask_rows(s2.at[u], m_out, (1 - core) * 24 + u * 12, slice(None))
        gives.append(remote(s2.at[u], w2.at[1, u], wsend_sem.at[2 * u], wrecv_sem.at[2 * u], sibling))
        gives[-1].start()
        loads[4 * u + 1].wait()
        mask_rows(s1.at[u], m_in.at[1], 0, columns)
        gives.append(remote(s1.at[u], w1.at[1, u], wsend_sem.at[2 * u + 1], wrecv_sem.at[2 * u + 1], sibling))
        gives[-1].start()

    for copy in a2a_copies:
        copy.wait_recv()
    for other, s in ((1, 0), (0, 7)):
        for pair in range(8):
            rows = []
            for c in (2 * pair, 2 * pair + 1):
                block = a2a_recv[other, c].astype(F32)
                rows.append(jnp.concatenate([block[:8], block[8:]], axis=1))
            xg[0, s, 0, pair * 16 : (pair + 1) * 16, :] = jnp.concatenate(rows, axis=0).astype(BF16)
        if other:
            group_copy(7, 0, 1, hop_mate).wait_recv()
            forward(0).start()
            for k in (0, 1):
                group_copy(0, 1, k, z_mate[0]).start()

    for u in (0, 1):
        loads[4 * u + 2].wait()
        mask_rows(w2.at[0, u], m_out, core * 24 + u * 12, slice(None))
        loads[4 * u + 3].wait()
        mask_rows(w1.at[0, u], m_in.at[0], 0, slice(u * COLS, (u + 1) * COLS))

    for give in gives[:2]:
        give.wait_recv()

    def choose(order, done, axis=None, own=True):
        where = [slice(None)] * 3
        if axis is not None:
            where[axis] = bit[axis] if own else 1 - bit[axis]
        return tuple(where[d] for d in range(3) if d not in order[:done])

    def sum_copies(n, stage):
        two, copies = n % 2, []
        source = (part_send, half_send, quarter_send)[stage]
        target = (half_recv, quarter_recv, eighth_recv)[stage]
        for i, ((low, high), order) in enumerate(RANGES):
            axis = order[stage]
            copies.append(
                remote(
                    source.at[(two, slice(None), *choose(order, stage, axis, False), slice(None), slice(low, high))],
                    target.at[n, ..., low:high],
                    sum_ss.at[stage, two, i], sum_rs.at[stage, n, i], mate[axis],
                )
            )
        return copies

    def gather_copies(n, stage):
        two, copies = n % 2, []
        for i, ((low, high), order) in enumerate(RANGES):
            where = tuple(bit[d] if d in order[: stage + 1] else slice(None) for d in range(3))
            block = ahg.at[(n, slice(None), *where, slice(None), slice(low, high))]
            copies.append(remote(block, block, gather_ss.at[stage, two, i], gather_rs.at[stage, n, i], mate[order[stage]]))
        return copies

    def received(n, stage, own):
        two = n % 2
        for copy in sum_copies(n, stage):
            copy.wait()
        arrived = (half_recv, quarter_recv, eighth_recv)[stage]
        for (low, high), order in RANGES:
            here = own[(two, slice(None), *choose(order, stage, order[stage]), slice(None), slice(low, high))]
            yield low, high, here + arrived[n, ..., low:high].astype(F32)

    def sib_copy(s):
        two = s % 2
        return remote(sib_send.at[two], sib_recv.at[s], sib_ss.at[two], sib_rs.at[s], sibling)

    def tokens_of(s):
        return pl.ds(pl.multiple_of(s * GROUP, GROUP), GROUP)

    def keep_copies(n):
        s, u, two = n // 2, n % 2, n % 2
        pairs = [(at_buf.at[two], at_out.at[core, u, :, tokens_of(s)]), (hg_buf.at[two], hg_out.at[core, u, tokens_of(s), :])]
        copies = []
        for k, (source, target) in enumerate(pairs):
            copies.append(pltpu.make_async_copy(source, target, keep_sem.at[two, k]))
            copies.append(remote(source, target, give_ss.at[two, k], give_rs.at[n, k], sibling))
        return copies

    def store_copies(s):
        return [
            pltpu.make_async_copy(xt_buf, xt_out.at[:, tokens_of(s)], store_sem.at[0]),
            pltpu.make_async_copy(xg.at[0, s, 1], g_out.at[tokens_of(s), :], store_sem.at[1]),
        ]

    def row_copy(s):
        two = s % 2
        by = jnp.where(s < 4, s, s - 3)
        return remote(row_send.at[two], row_recv.at[s], row_ss.at[two], row_rs.at[s], (flip(z, by) * 2 + xh, col))

    def multiply(n):
        s, u, two = n // 2, n % 2, n % 2

        @pl.when(u == 0)
        def _():
            forward(s).wait_recv()

        @pl.when(n == 1)
        def _():
            for give in gives[2:]:
                give.wait_recv()

        for j in range(COLS // TILE):
            here = slice(j * TILE, (j + 1) * TILE)
            total = lax.dot_general(xg[0, s, 1], w2[0, u, here, :], NT, preferred_element_type=F32)
            total += lax.dot_general(xg[1, s, 1], w2[1, u, here, :], NT, preferred_element_type=F32)
            total = total.reshape(2, 2, 2, 16, TILE)
            part[two, 1, ..., here] = total
            part_send[two, 1, ..., here] = total.astype(BF16)
        for j in range(COLS // TILE):
            here = slice(j * TILE, (j + 1) * TILE)
            total = jnp.dot(xg[0, s, 0], w1[0, u, :, here], preferred_element_type=F32)
            total += jnp.dot(xg[1, s, 0], w1[1, u, :, here], preferred_element_type=F32)
            total = total.reshape(2, 2, 2, 16, TILE)
            part[two, 0, ..., here] = total
            part_send[two, 0, ..., here] = total.astype(BF16)
        for copy in sum_copies(n, 0):
            copy.start()

    def receive(s):
        @pl.when(s < GROUPS - 1)
        def _():
            for k in (0, 1):
                group_copy(7, s, k, hop_mate).wait_recv()

        forward(s).start()

    def relay(t):
        for at, source, target, d in ((0, 0, 2, 2), (2, 0, 3, 3), (3, 7, 4, 1), (5, 7, 5, 2), (7, 7, 6, 3)):

            @pl.when(t == at)
            def _(source=source, target=target, d=d):
                for k in (0, 1):
                    group_copy(source, target, k, z_mate[d - 1]).start()

    def add_half(n):
        for low, high, total in received(n, 0, part):
            half[n % 2, ..., low:high] = total
            half_send[n % 2, ..., low:high] = total.astype(BF16)
        for copy in sum_copies(n, 1):
            copy.start()

    def add_quarter(n):
        for low, high, total in received(n, 1, half):
            quarter[n % 2, ..., low:high] = total
            quarter_send[n % 2, ..., low:high] = total.astype(BF16)
        for copy in sum_copies(n, 2):
            copy.start()

    def activate(n):
        for low, high, total in received(n, 2, quarter):
            for k, values in enumerate(gelu_parts(total[0], total[1])):
                ahg[n, k, bit[0], bit[1], bit[2], :, low:high] = values.astype(BF16)
        for copy in gather_copies(n, 2):
            copy.start()

    def spread(n, stage):
        for copy in gather_copies(n, stage + 1):
            copy.wait()
        for copy in gather_copies(n, stage):
            copy.start()

    def project(n):
        s, u, two = n // 2, n % 2, (n // 2) % 2
        for copy in gather_copies(n, 0):
            copy.wait()
        hg_buf[n % 2] = ahg[n, 1].reshape(GROUP, COLS)

        def products(fc, here):
            activated, hidden_grad = (ahg[n, k].reshape(GROUP, COLS) for k in (0, 1))
            return (
                jnp.dot(activated, w2[fc, u, :, here], preferred_element_type=F32),
                lax.dot_general(hidden_grad, w1[fc, u, here, :], NT, preferred_element_type=F32),
            )

        @pl.when(u == 0)
        def _():
            for fc in (1, 0):
                for j in range(FEAT // TILE):
                    here = slice(j * TILE, (j + 1) * TILE)
                    for k, value in enumerate(products(fc, here)):
                        prod[two, fc, k, :, here] = value

        @pl.when(u == 1)
        def _():
            for j in range(FEAT // TILE):
                here = slice(j * TILE, (j + 1) * TILE)
                for k, value in enumerate(products(1, here)):
                    sib_send[two, k, :, here] = (prod[two, 1, k, :, here] + value).astype(BF16)
            sib_copy(s).start()
            for j in range(FEAT // TILE):
                here = slice(j * TILE, (j + 1) * TILE)
                for k, value in enumerate(products(0, here)):
                    prod[two, 0, k, :, here] += value

        at_buf[n % 2] = ahg[n, 0].reshape(GROUP, COLS).T
        for copy in keep_copies(n):
            copy.start()

        @pl.when(u == 0)
        def _():
            xt_buf[...] = xg[0, s, 0].T
            for copy in store_copies(s):
                copy.start()

    def hand_on(n):
        s, two = n // 2, (n // 2) % 2

        @pl.when(n % 2 == 1)
        def _():
            sib_copy(s).wait()

            @pl.when(jnp.logical_or(s == 0, s == 7))
            def _():
                row_own[jnp.where(s == 0, 1, 0)] = prod[two, 0] + sib_recv[s].astype(F32)

            @pl.when(jnp.logical_and(s != 0, s != 7))
            def _():
                row_send[two] = (prod[two, 0] + sib_recv[s].astype(F32)).astype(BF16)
                row_copy(s).start()

    def finish(n):
        s = n // 2
        for copy in keep_copies(n):
            copy.wait()

        @pl.when(n % 2 == 0)
        def _():
            for copy in store_copies(s):
                copy.wait()

    def settle(n):
        s = n // 2

        @pl.when(jnp.logical_and(n % 2 == 1, jnp.logical_and(s != 0, s != 7)))
        def _():
            row_copy(s).wait_send()

    def hop_copy(k, i):
        rows = slice(i * 32, (i + 1) * 32)
        return remote(hop_send.at[k, rows], hop_recv.at[k, rows], hop_ss.at[k, i], hop_rs.at[k, i], hop_mate)

    def step(t, carry):
        def at(lag, stage):
            pl.when(jnp.logical_and(t >= lag, t < UNITS + lag))(lambda: stage(t - lag))

        at(0, multiply)
        at(1, add_half)
        at(2, add_quarter)
        at(3, activate)
        at(4, lambda n: spread(n, 1))
        at(5, lambda n: spread(n, 0))

        pl.when(t < 8)(lambda: relay(t))

        @pl.when(jnp.logical_and(t % 2 == 1, t < UNITS - 2))
        def _():
            receive(t // 2 + 1)

        at(7, finish)
        at(6, project)
        at(9, settle)
        at(7, hand_on)

        @pl.when(t == 16)
        def _():
            total = row_own[1]
            for s in (1, 2, 3):
                row_copy(s).wait_recv()
                total += row_recv[s].astype(F32)
            hop_send[...] = total.astype(BF16)

        for i in range(4):

            @pl.when(t == 16 + i)
            def _(i=i):
                for k in (0, 1):
                    hop_copy(k, i).start()

        return carry

    lax.fori_loop(0, UNITS + 7, step, 0)

    total = row_own[0]
    for s in (4, 5, 6):
        row_copy(s).wait_recv()
        total += row_recv[s].astype(F32)
    for i in range(4):
        for k in (0, 1):
            hop_copy(k, i).wait()
    total += hop_recv[...].astype(F32)
    out_ref[...] = total[0].astype(BF16)
    ig_ref[...] = total[1].astype(BF16)

    for give in gives:
        give.wait_send()
    for copy in a2a_copies:
        copy.wait_send()
    for s in range(GROUPS):
        forward(s).wait_send()
    for s in range(GROUPS - 1):
        for k in (0, 1):
            if s or k:
                group_copy(7, s, k, hop_mate).wait_send()


def run_pipeline(inputs, cotangent, w_in, w_out, mask_in, mask_out):
    vmem = pl.BlockSpec(memory_space=pltpu.VMEM)
    hbm = pl.BlockSpec(memory_space=pltpu.HBM)
    dma = pltpu.SemaphoreType.DMA
    tokens = GROUP * GROUPS
    return pl.pallas_call(
        pipeline,
        out_shape=[
            jax.ShapeDtypeStruct((GROUP, FEAT), BF16),
            jax.ShapeDtypeStruct((GROUP, FEAT), BF16),
            jax.ShapeDtypeStruct((FEAT, tokens), BF16),
            jax.ShapeDtypeStruct((tokens, FEAT), BF16),
            jax.ShapeDtypeStruct((2, 2, COLS, tokens), BF16),
            jax.ShapeDtypeStruct((2, 2, tokens, COLS), BF16),
        ],
        in_specs=[vmem, hbm, hbm, hbm, vmem, vmem],
        out_specs=[vmem, vmem, hbm, hbm, hbm, hbm],
        scratch_shapes=[
            pltpu.VMEM((2, 2, FEAT, COLS), BF16),
            pltpu.VMEM((2, 2, COLS, FEAT), BF16),
            pltpu.VMEM((2, FEAT, COLS), BF16),
            pltpu.VMEM((2, COLS, FEAT), BF16),
            pltpu.VMEM((2, 12, 2 * COLS), F32),
            pltpu.VMEM((48, FEAT), F32),
            pltpu.VMEM((16, 16, FEAT // 2), BF16),
            pltpu.VMEM((2, 16, 16, FEAT // 2), BF16),
            pltpu.VMEM((2, GROUPS, 2, GROUP, FEAT), BF16),
            pltpu.VMEM((2, 2, 2, 2, 2, 16, COLS), F32),
            pltpu.VMEM((2, 2, 2, 2, 2, 16, COLS), BF16),
            pltpu.VMEM((2, 2, 2, 2, 16, COLS), F32),
            pltpu.VMEM((2, 2, 2, 2, 16, COLS), BF16),
            pltpu.VMEM((2, 2, 2, 16, COLS), F32),
            pltpu.VMEM((2, 2, 2, 16, COLS), BF16),
            pltpu.VMEM((UNITS, 2, 2, 2, 16, COLS), BF16),
            pltpu.VMEM((UNITS, 2, 2, 16, COLS), BF16),
            pltpu.VMEM((UNITS, 2, 16, COLS), BF16),
            pltpu.VMEM((UNITS, 2, 2, 2, 2, 16, COLS), BF16),
            pltpu.VMEM((2, 2, 2, GROUP, FEAT), F32),
            pltpu.VMEM((2, 2, GROUP, FEAT), BF16),
            pltpu.VMEM((GROUPS, 2, GROUP, FEAT), BF16),
            pltpu.VMEM((2, 2, GROUP, FEAT), BF16),
            pltpu.VMEM((GROUPS, 2, GROUP, FEAT), BF16),
            pltpu.VMEM((2, 2, GROUP, FEAT), F32),
            pltpu.VMEM((2, GROUP, FEAT), BF16),
            pltpu.VMEM((2, GROUP, FEAT), BF16),
            pltpu.VMEM((2, COLS, GROUP), BF16),
            pltpu.VMEM((2, GROUP, COLS), BF16),
            pltpu.VMEM((FEAT, GROUP), BF16),
            dma((9,)), dma((4,)), dma((4,)),
            dma((2, 16)), dma((2, 16)),
            dma((GROUPS, 2)), dma((GROUPS, 2)), dma((GROUPS,)), dma((GROUPS,)),
            dma((3, 2, 4)), dma((3, UNITS, 4)), dma((3, 2, 4)), dma((3, UNITS, 4)),
            dma((2,)), dma((GROUPS,)), dma((2,)), dma((GROUPS,)),
            dma((2, 2)), dma((2, 2)), dma((UNITS, 2)), dma((2,)),
            dma((2, 4)), dma((2, 4)),
        ],
        compiler_params=pltpu.CompilerParams(
            collective_id=1, has_side_effects=True, vmem_limit_bytes=60 << 20
        ),
        cost_estimate=pl.CostEstimate(flops=20 << 30, bytes_accessed=30 << 20, transcendentals=1 << 20),
    )(inputs, cotangent, w_in, w_out, mask_in, mask_out)


def weight_grads(
    xt_ref, g_ref, at_ref, hg_ref, mask_in_ref, mask_out_ref, out_in, ig_in, w_in_ref, w_out_ref, out_ref, ig_ref
):
    j = pl.program_id(0)

    @pl.when(j == 0)
    def _():
        out_ref[...] = out_in[...]
        ig_ref[...] = ig_in[...]

    mask = mask_in_ref[...].astype(F32).astype(BF16)
    keep_in = jnp.dot(mask, one_hot((48, COLS), 1, 6, j * (COLS // 64)), preferred_element_type=F32)
    mask = mask_out_ref[...].astype(F32).astype(BF16)
    rows = lax.dot_general(one_hot((12, 48), 0, 0, j * 12), mask, NT, preferred_element_type=F32).astype(BF16)
    keep_out = jnp.dot(rows, one_hot((12, FEAT), 1, 6, 0), preferred_element_type=F32)

    for left, right, keep, result in ((xt_ref, hg_ref, keep_in, w_in_ref), (at_ref, g_ref, keep_out, w_out_ref)):
        for r in range(FEAT // TILE):
            product = jnp.dot(left[r * TILE : (r + 1) * TILE, :], right[...], preferred_element_type=F32)
            for i in range(TILE // 64):
                b = r * (TILE // 64) + i
                value = product[i * 64 : (i + 1) * 64, :] * keep[b : b + 1, :]
                result[b * 64 : (b + 1) * 64, :] = value.astype(BF16)


def run_weight_grads(output, input_grad, xt, g, at, hg, mask_in, mask_out):
    tokens = GROUP * GROUPS

    def whole(*shape):
        return pl.BlockSpec(shape, lambda j: (0, 0))

    def tile(*shape):
        return pl.BlockSpec((None, None, *shape), lambda j: (j // 2, j % 2, 0, 0))

    return pl.pallas_call(
        weight_grads,
        grid=(4,),
        out_shape=[
            jax.ShapeDtypeStruct((FEAT, 4 * COLS), BF16),
            jax.ShapeDtypeStruct((4 * COLS, FEAT), BF16),
            jax.ShapeDtypeStruct((GROUP, FEAT), BF16),
            jax.ShapeDtypeStruct((GROUP, FEAT), BF16),
        ],
        in_specs=[
            whole(FEAT, tokens), whole(tokens, FEAT), tile(COLS, tokens), tile(tokens, COLS),
            whole(12, 48), whole(12, 48), whole(GROUP, FEAT), whole(GROUP, FEAT),
        ],
        out_specs=[
            pl.BlockSpec((FEAT, COLS), lambda j: (0, j)), pl.BlockSpec((COLS, FEAT), lambda j: (j, 0)),
            whole(GROUP, FEAT), whole(GROUP, FEAT),
        ],
        compiler_params=pltpu.CompilerParams(vmem_limit_bytes=60 << 20),
        cost_estimate=pl.CostEstimate(flops=10 << 30, bytes_accessed=25 << 20, transcendentals=0),
    )(xt, g, at, hg, mask_in, mask_out, output, input_grad)


def body(inputs, cotangent, w_in, w_out, mask_in, mask_out):
    mask_out = mask_out.T
    made = run_pipeline(inputs, cotangent, w_in, w_out, mask_in, mask_out)
    w_in_grad, w_out_grad, output, input_grad = run_weight_grads(*made, mask_in, mask_out)
    return (output, input_grad, w_in_grad, w_out_grad)


def solution(mesh):
    in_specs = (
        P(("row", "col"), None),
        P("row", "col"),
        P("col", "row"),
        P("row", "col"),
        P("col", "row"),
        P("row", "col"),
    )
    out_specs = (P("row", "col"), P("row", "col"), P("col", "row"), P("row", "col"))
    return jax.shard_map(body, mesh=mesh, in_specs=in_specs, out_specs=out_specs, check_vma=False)
```

time: 170 us -> 158 us (0.929)
  Pallas kernels: 168 us -> 157 us
    pallas_call x1, Pallas kernels: 150 us -> 142 us  [run_pipeline(): pl.pallas_call(pipeline, out_shape=[jax.ShapeDtypeStruct((GROUP, FEAT), B...]
    pallas_call x1, Pallas kernels: 17.8 us -> 15.1 us  [run_weight_grads(): pl.pallas_call(weight_grads, grid=(4,), out_shape=[jax.ShapeDtypeStruct((...]
where the time goes in v3:
time: 158 us; the launch traced here: 157 us
  Pallas kernels  157 us (99%)
    pallas_call x1, Pallas kernels, run_pipeline(): pl.pallas_call(pipeline, out_shape=[jax.ShapeDtypeStruct((GROUP, FEAT), B...  142 us
    pallas_call x1, Pallas kernels, run_weight_grads(): pl.pallas_call(weight_grads, grid=(4,), out_shape=[jax.ShapeDtypeStruct((...  15.1 us

profile of v3, /device:TPU:0, one launch (start us, length us, event | category | flops | bytes accessed | tf_op | source)
XLA Modules:
  0.0 157.4 jit_solution(7518776296037314400)
XLA Ops:
  0.6 141.6 %shard_map.93 = (bf16[128,768]{1,0:T(8,128)(2,1)}, bf16[128,768]{1,0:T(8,128)(2,1)}, bf16[768,1024]{1,0:T(8,128)(2,1)}, bf16[1024,768]{1,0:T(8,128)(2,1)}, bf16[...) custom-call(bf16[8,12288]{1,0:T(8,128)(2,1)} %inputs_ref.1, bf16[128,768]{1,0:T(8,128)(2,1)} %cot_ref.1, ...), custom_call_target="tpu_custom_call" | custom-call | flops 21474836480 | bytes 31457280 | tf_op jit(solution)/shard_map/pallas_call | solution.py:455
  142.2 15.1 %shard_map.94 = (bf16[768,3072]{1,0:T(8,128)(2,1)}, bf16[3072,768]{1,0:T(8,128)(2,1)}, bf16[128,768]{1,0:T(8,128)(2,1)}, bf16[128,768]{1,0:T(8,128)(2,1)}) custom-call(bf16[768,1024]{1,0:T(8,128)(2,1)} %get-tuple-element.14.xt_ref, bf16[1024,768]{1,0:T(8,128)(2,1)} %get-tuple-element.15.g_ref, bf16[2,2,768,1024]{3,2,1,0:T(8,128)(2,1)} %get-tuple-element.16.at_ref, ...), custom_call_target="tpu_custom_call" | custom-call | flops 10737418240 | bytes 26214400 | tf_op jit(solution)/shard_map/pallas_call | solution.py:547

commit v4 on v3

--- a/solution.py
+++ b/solution.py
@@ -102,9 +102,10 @@
         device = (near if other else row, to)
         return remote(a2a_send.at[to], a2a_recv.at[other, col], a_ssem.at[other, d], a_rsem.at[other, d], device)
 
-    a2a_copies = [a2a_copy(d, 1) for d in range(16)] + [a2a_copy(d, 0) for d in range(1, 16)]
-    for copy in a2a_copies:
-        copy.start()
+    a2a_copies = [[a2a_copy(d, other) for d in range(16) if other or d] for other in range(2)]
+    for other in (1, 0):
+        for copy in a2a_copies[other]:
+            copy.start()
     a2a_recv[0, col] = a2a_send[col]
 
     def group_copy(source, target, k, device):
@@ -142,20 +143,21 @@
         gives.append(remote(s1.at[u], w1.at[1, u], wsend_sem.at[2 * u + 1], wrecv_sem.at[2 * u + 1], sibling))
         gives[-1].start()
 
-    for copy in a2a_copies:
-        copy.wait_recv()
-    for other, s in ((1, 0), (0, 7)):
+    def assemble(other, s):
+        for copy in a2a_copies[other]:
+            copy.wait_recv()
         for pair in range(8):
             rows = []
             for c in (2 * pair, 2 * pair + 1):
                 block = a2a_recv[other, c].astype(F32)
                 rows.append(jnp.concatenate([block[:8], block[8:]], axis=1))
             xg[0, s, 0, pair * 16 : (pair + 1) * 16, :] = jnp.concatenate(rows, axis=0).astype(BF16)
-        if other:
-            group_copy(7, 0, 1, hop_mate).wait_recv()
-            forward(0).start()
-            for k in (0, 1):
-                group_copy(0, 1, k, z_mate[0]).start()
+
+    assemble(1, 0)
+    group_copy(7, 0, 1, hop_mate).wait_recv()
+    forward(0).start()
+    for k in (0, 1):
+        group_copy(0, 1, k, z_mate[0]).start()
 
     for u in (0, 1):
         loads[4 * u + 2].wait()
@@ -269,6 +271,8 @@
         forward(s).start()
 
     def relay(t):
+        pl.when(t == 0)(lambda: assemble(0, 7))
+
         for at, source, target, d in ((0, 0, 2, 2), (2, 0, 3, 3), (3, 7, 4, 1), (5, 7, 5, 2), (7, 7, 6, 3)):
 
             @pl.when(t == at)
@@ -393,6 +397,8 @@
         at(3, activate)
         at(4, lambda n: spread(n, 1))
         at(5, lambda n: spread(n, 0))
+        at(9, settle)
+        at(7, hand_on)
 
         pl.when(t < 8)(lambda: relay(t))
 
@@ -402,8 +408,6 @@
 
         at(7, finish)
         at(6, project)
-        at(9, settle)
-        at(7, hand_on)
 
         @pl.when(t == 16)
         def _():
@@ -437,8 +441,9 @@
 
     for give in gives:
         give.wait_send()
-    for copy in a2a_copies:
-        copy.wait_send()
+    for copies in a2a_copies:
+        for copy in copies:
+            copy.wait_send()
     for s in range(GROUPS):
         forward(s).wait_send()
     for s in range(GROUPS - 1):

time: 158 us -> 155 us (0.981)
  Pallas kernels: 157 us -> 154 us
    pallas_call x1, Pallas kernels: 142 us -> 139 us  [run_pipeline(): pl.pallas_call(pipeline, out_shape=[jax.ShapeDtypeStruct((GROUP, FEAT), B...]
where the time goes in v4:
time: 155 us
  Pallas kernels  154 us (99%)
    pallas_call x1, Pallas kernels, run_pipeline(): pl.pallas_call(pipeline, out_shape=[jax.ShapeDtypeStruct((GROUP, FEAT), B...  139 us
    pallas_call x1, Pallas kernels, run_weight_grads(): pl.pallas_call(weight_grads, grid=(4,), out_shape=[jax.ShapeDtypeStruct((...  15.1 us

profile of v4, /device:TPU:0, one launch (start us, length us, event | category | flops | bytes accessed | tf_op | source)
XLA Modules:
  0.0 154.6 jit_solution(16060335581221787308)
XLA Ops:
  0.6 138.8 %shard_map.93 = (bf16[128,768]{1,0:T(8,128)(2,1)}, bf16[128,768]{1,0:T(8,128)(2,1)}, bf16[768,1024]{1,0:T(8,128)(2,1)}, bf16[1024,768]{1,0:T(8,128)(2,1)}, bf16[...) custom-call(bf16[8,12288]{1,0:T(8,128)(2,1)} %inputs_ref.1, bf16[128,768]{1,0:T(8,128)(2,1)} %cot_ref.1, ...), custom_call_target="tpu_custom_call" | custom-call | flops 21474836480 | bytes 31457280 | tf_op jit(solution)/shard_map/pallas_call | solution.py:460
  139.5 15.1 %shard_map.94 = (bf16[768,3072]{1,0:T(8,128)(2,1)}, bf16[3072,768]{1,0:T(8,128)(2,1)}, bf16[128,768]{1,0:T(8,128)(2,1)}, bf16[128,768]{1,0:T(8,128)(2,1)}) custom-call(bf16[768,1024]{1,0:T(8,128)(2,1)} %get-tuple-element.14.xt_ref, bf16[1024,768]{1,0:T(8,128)(2,1)} %get-tuple-element.15.g_ref, bf16[2,2,768,1024]{3,2,1,0:T(8,128)(2,1)} %get-tuple-element.16.at_ref, ...), custom_call_target="tpu_custom_call" | custom-call | flops 10737418240 | bytes 26214400 | tf_op jit(solution)/shard_map/pallas_call | solution.py:552

commit v5 on v4

--- a/solution.py
+++ b/solution.py
@@ -153,17 +153,17 @@
                 rows.append(jnp.concatenate([block[:8], block[8:]], axis=1))
             xg[0, s, 0, pair * 16 : (pair + 1) * 16, :] = jnp.concatenate(rows, axis=0).astype(BF16)
 
-    assemble(1, 0)
-    group_copy(7, 0, 1, hop_mate).wait_recv()
-    forward(0).start()
-    for k in (0, 1):
-        group_copy(0, 1, k, z_mate[0]).start()
-
     for u in (0, 1):
         loads[4 * u + 2].wait()
         mask_rows(w2.at[0, u], m_out, core * 24 + u * 12, slice(None))
         loads[4 * u + 3].wait()
         mask_rows(w1.at[0, u], m_in.at[0], 0, slice(u * COLS, (u + 1) * COLS))
+
+    group_copy(7, 0, 1, hop_mate).wait_recv()
+    group_copy(0, 1, 1, z_mate[0]).start()
+    assemble(1, 0)
+    forward(0).start()
+    group_copy(0, 1, 0, z_mate[0]).start()
 
     for give in gives[:2]:
         give.wait_recv()
@@ -532,10 +532,10 @@
     keep_out = jnp.dot(rows, one_hot((12, FEAT), 1, 6, 0), preferred_element_type=F32)
 
     for left, right, keep, result in ((xt_ref, hg_ref, keep_in, w_in_ref), (at_ref, g_ref, keep_out, w_out_ref)):
-        for r in range(FEAT // TILE):
-            product = jnp.dot(left[r * TILE : (r + 1) * TILE, :], right[...], preferred_element_type=F32)
-            for i in range(TILE // 64):
-                b = r * (TILE // 64) + i
+        for r in range(2):
+            product = jnp.dot(left[r * 384 : (r + 1) * 384, :], right[...], preferred_element_type=F32)
+            for i in range(6):
+                b = r * 6 + i
                 value = product[i * 64 : (i + 1) * 64, :] * keep[b : b + 1, :]
                 result[b * 64 : (b + 1) * 64, :] = value.astype(BF16)
 

time: 155 us -> 155 us (level)
  no operation moved by 1% of the time
where the time goes in v5:
time: 155 us
  Pallas kernels  154 us (99%)
    pallas_call x1, Pallas kernels, run_pipeline(): pl.pallas_call(pipeline, out_shape=[jax.ShapeDtypeStruct((GROUP, FEAT), B...  139 us
    pallas_call x1, Pallas kernels, run_weight_grads(): pl.pallas_call(weight_grads, grid=(4,), out_shape=[jax.ShapeDtypeStruct((...  15.1 us

profile of v5, /device:TPU:0, one launch (start us, length us, event | category | flops | bytes accessed | tf_op | source)
XLA Modules:
  0.0 154.6 jit_solution(17773525701252571574)
XLA Ops:
  0.6 138.8 %shard_map.93 = (bf16[128,768]{1,0:T(8,128)(2,1)}, bf16[128,768]{1,0:T(8,128)(2,1)}, bf16[768,1024]{1,0:T(8,128)(2,1)}, bf16[1024,768]{1,0:T(8,128)(2,1)}, bf16[...) custom-call(bf16[8,12288]{1,0:T(8,128)(2,1)} %inputs_ref.1, bf16[128,768]{1,0:T(8,128)(2,1)} %cot_ref.1, ...), custom_call_target="tpu_custom_call" | custom-call | flops 21474836480 | bytes 31457280 | tf_op jit(solution)/shard_map/pallas_call | solution.py:460
  139.5 15.1 %shard_map.94 = (bf16[768,3072]{1,0:T(8,128)(2,1)}, bf16[3072,768]{1,0:T(8,128)(2,1)}, bf16[128,768]{1,0:T(8,128)(2,1)}, bf16[128,768]{1,0:T(8,128)(2,1)}) custom-call(bf16[768,1024]{1,0:T(8,128)(2,1)} %get-tuple-element.14.xt_ref, bf16[1024,768]{1,0:T(8,128)(2,1)} %get-tuple-element.15.g_ref, bf16[2,2,768,1024]{3,2,1,0:T(8,128)(2,1)} %get-tuple-element.16.at_ref, ...), custom_call_target="tpu_custom_call" | custom-call | flops 10737418240 | bytes 26214400 | tf_op jit(solution)/shard_map/pallas_call | solution.py:552
